TPU v7x, 32 devices: a whole 2x2x4 slice. The times are simulated.
32 devices in a mesh: groups: 2 (over y), row: 4 (over z), col: 4 (over x, core).
Axes of the slice: x: 2, y: 2, z: 4, core: 2. Of those that a mesh axis runs over, the one named last changes fastest.
Arguments:
- x_points: float32 [8192, 32], P(('groups', 'row')), parts along dimension 0, may hold values from -3 to 3
- y_points: float32 [8192, 32], P(('groups', 'col')), parts along dimension 0, may hold values from -3 to 3
Outputs:
- grad_x: float32 [8192, 32], P(('groups', 'row', 'col')), parts along dimension 0
- grad_y: float32 [8192, 32], P(('groups', 'col', 'row')), parts along dimension 0
There are 2 independent parts, one for each index of `groups`. A program takes and returns all parts, laid end to end along the dimension named above; each array names one. Nothing has to cross between parts.
All inputs are finite; a program needn't handle non-finite values.
Results may differ from a plain program's by a relative error of at most 0.0003.
Values sent between devices are 32-bit elements; how exact they have to be, the bound alone decides.
No kernel may reach another device: no remote copies, remote signals or barrier semaphores. Data moves between devices by JAX's collectives and lax.ppermute only.
A program may use at most 64 MiB of HBM per device.

v0:
```python
import math

import jax
import jax.numpy as jnp
from jax import lax
from jax.sharding import PartitionSpec as P

ITERS = 5


EPSILON = 0.05
HIGHEST = lax.Precision.HIGHEST


def pair_cost(row_pts, col_pts):
    sq_rows = jnp.sum(row_pts * row_pts, axis=1)
    sq_cols = jnp.sum(col_pts * col_pts, axis=1)
    inner_prod = lax.dot_general(
        row_pts,
        col_pts,
        (((1,), (1,)), ((), ())),
        precision=HIGHEST,
        preferred_element_type=jnp.float32,
    )
    return sq_rows[:, None] + sq_cols[None, :] - 2.0 * inner_prod


def reduce_lse(maxima, totals, across):
    if across == "col":
        highest = lax.pmax(maxima, "col")
        totals = lax.psum(totals * jnp.exp(maxima - highest), "col")
        maxima = highest
    else:
        highest = lax.pmax(maxima, "row")
        totals = lax.psum(totals * jnp.exp(maxima - highest), "row")
        maxima = highest
    return maxima + jnp.log(totals)


def split_blocks(array, width):
    return array.reshape((array.shape[0] // width, width) + array.shape[1:])


def row_update(x_local, y_local, pot_cols, width, log_mass):
    count_rows = x_local.shape[0]

    def row_advance(carry, pieces):
        maxima, totals = carry
        y_block, pot_block = pieces
        scores = (pot_block[None, :] - pair_cost(x_local, y_block)) / EPSILON
        fresh = jnp.maximum(maxima, jnp.max(scores, axis=1))
        totals = totals * jnp.exp(maxima - fresh) + jnp.sum(
            jnp.exp(scores - fresh[:, None]), axis=1
        )
        return ((fresh, totals), None)

    start = (jnp.full((count_rows,), -jnp.inf, jnp.float32), jnp.zeros((count_rows,), jnp.float32))
    (maxima, totals), unused = lax.scan(
        row_advance, start, (split_blocks(y_local, width), split_blocks(pot_cols, width))
    )
    return EPSILON * log_mass - EPSILON * reduce_lse(maxima, totals, "col")


def col_update(x_local, y_local, pot_rows, width, log_mass):

    def col_advance(carry, y_block):
        scores = (pot_rows[:, None] - pair_cost(x_local, y_block)) / EPSILON
        maxima = jnp.max(scores, axis=0)
        totals = jnp.sum(jnp.exp(scores - maxima[None, :]), axis=0)
        return (carry, (maxima, totals))

    unused, (maxima, totals) = lax.scan(col_advance, jnp.float32(0.0), split_blocks(y_local, width))
    return EPSILON * log_mass - EPSILON * reduce_lse(maxima.reshape(-1), totals.reshape(-1), "row")


def adjoint_pass(x_local, y_local, pot_rows, pot_cols, scale, row_weight, col_weight, width):
    count_rows = x_local.shape[0]

    def adjoint_advance(carry, pieces):
        row_acc, grad_acc = carry
        y_block, pot_block, weight_block = pieces
        weights = (
            scale
            * jnp.exp(
                (pot_rows[:, None] + pot_block[None, :] - pair_cost(x_local, y_block)) / EPSILON
            )
            * row_weight[:, None]
            * weight_block[None, :]
        )
        row_acc = row_acc + jnp.sum(weights, axis=1)
        grad_acc = grad_acc + jnp.dot(
            weights, y_block, precision=HIGHEST, preferred_element_type=jnp.float32
        )
        col_part = jnp.sum(weights, axis=0)
        grad_cols = lax.dot_general(
            weights,
            x_local,
            (((0,), (0,)), ((), ())),
            precision=HIGHEST,
            preferred_element_type=jnp.float32,
        )
        return ((row_acc, grad_acc), (col_part, grad_cols))

    start = (jnp.zeros((count_rows,), jnp.float32), jnp.zeros(x_local.shape, jnp.float32))
    pieces = (
        split_blocks(y_local, width),
        split_blocks(pot_cols, width),
        split_blocks(col_weight, width),
    )
    (row_acc, grad_acc), (col_part, grad_cols) = lax.scan(adjoint_advance, start, pieces)
    return (row_acc, grad_acc, col_part.reshape(-1), grad_cols.reshape(y_local.shape))


def on_device(x_points, y_points):
    count_rows = x_points.shape[0]
    count_cols = y_points.shape[0]
    width = min(128, count_cols)
    total_rows = count_rows * lax.axis_size("row")
    total_cols = count_cols * lax.axis_size("col")
    log_rows_mass = -math.log(total_rows)
    log_cols_mass = -math.log(total_cols)
    pot_cols = jnp.zeros((count_cols,), jnp.float32)
    history_rows = []
    history_cols = [pot_cols]
    for level in range(ITERS):
        pot_rows = row_update(x_points, y_points, pot_cols, width, log_rows_mass)
        pot_cols = col_update(x_points, y_points, pot_rows, width, log_cols_mass)
        history_rows.append(pot_rows)
        history_cols.append(pot_cols)
    ones_rows = jnp.ones((count_rows,), jnp.float32)
    ones_cols = jnp.ones((count_cols,), jnp.float32)
    adj_cols = ones_cols
    rows_total = jnp.zeros((count_rows,), jnp.float32)
    cols_total = jnp.zeros((count_cols,), jnp.float32)
    grad_rows_acc = jnp.zeros(x_points.shape, jnp.float32)
    grad_cols_acc = jnp.zeros(y_points.shape, jnp.float32)
    for level in reversed(range(ITERS)):
        row_part, grad_part, col_part, grad_col_part = adjoint_pass(
            x_points,
            y_points,
            history_rows[level],
            history_cols[level + 1],
            float(total_cols),
            ones_rows,
            adj_cols,
            width,
        )
        rows_total = rows_total + row_part
        cols_total = cols_total + col_part
        grad_rows_acc = grad_rows_acc + grad_part
        grad_cols_acc = grad_cols_acc + grad_col_part
        leading = 1.0 if level == ITERS - 1 else 0.0
        adj_rows = leading - lax.psum(row_part, "col")
        row_part, grad_part, col_part, grad_col_part = adjoint_pass(
            x_points,
            y_points,
            history_rows[level],
            history_cols[level],
            float(total_rows),
            adj_rows,
            ones_cols,
            width,
        )
        rows_total = rows_total + row_part
        cols_total = cols_total + col_part
        grad_rows_acc = grad_rows_acc + grad_part
        grad_cols_acc = grad_cols_acc + grad_col_part
        if level > 0:
            adj_cols = -lax.psum(col_part, "row")
    part_x = 2.0 * (x_points * rows_total[:, None] - grad_rows_acc)
    part_y = 2.0 * (y_points * cols_total[:, None] - grad_cols_acc)
    whole_x = lax.psum(part_x, "col")
    share_x = count_rows // lax.axis_size("col")
    grad_x = lax.dynamic_slice_in_dim(whole_x, lax.axis_index("col") * share_x, share_x, 0)
    whole_y = lax.psum(part_y, "row")
    share_y = count_cols // lax.axis_size("row")
    grad_y = lax.dynamic_slice_in_dim(whole_y, lax.axis_index("row") * share_y, share_y, 0)
    return (grad_x, grad_y)


def solution(mesh):
    in_specs = (P(("groups", "row"), None), P(("groups", "col"), None))
    out_specs = (P(("groups", "row", "col"), None), P(("groups", "col", "row"), None))
    return jax.shard_map(
        on_device, mesh=mesh, in_specs=in_specs, out_specs=out_specs, check_vma=False
    )
```

profile of v0, /device:TPU:0, one launch (start us, length us, event | category | flops | bytes accessed | tf_op | source)
XLA Modules:
  0.0 677.6 jit_solution(13028964027017248017)
XLA Ops:
  30.3 9.3 %while.335 = (s32[]{:T(128)}, f32[8,128]{1,0:T(8,128)S(1)}, f32[8,128]{1,0:T(8,128)S(1)}, f32[1024]{0:T(1024)S(1)}, f32[1024]{0:T(1024)S(1)}, /*index=5*/f32[8,1...) while((s32[]{:T(128)}, f32[8,128]{1,0:T(8,128)S(1)}, f32[8,128]{1,0:T(8,128)S(1)}, ...), condition=%wide.region_12.13_spmd, body=%wide.region_8.12_spmd.sunk | while | flops 51388032 | bytes 1274477 | solution.py:72
  39.6 12.1 %pmax.71 = f32[1024]{0:T(1024)S(1)} all-reduce(f32[1024]{0:T(1024)S(1)} %bitcast.903), channel_id=1, replica_groups=mesh['groups'=2,'row'=4,'col'=4] {'row'}, use_global_device_ids=true, to_apply=%region_13.14 | all-reduce | flops 1024 | bytes 8192 | tf_op jit(solution)/shard_map/pmax | solution.py:34
  51.7 8.4 %psum.148 = f32[1024]{0:T(1024)S(1)} all-reduce(f32[1024]{0:T(1024)S(1)} %bitcast_multiply_fusion.24), channel_id=1, replica_groups=mesh['groups'=2,'row'=4,'col'=4] {'row'}, use_global_device_ids=true, to_apply=%region_14.15 | all-reduce | flops 1024 | bytes 8192 | tf_op jit(solution)/shard_map/psum | solution.py:35
  60.7 13.0 %while.341 = (s32[]{:T(128)}, f32[1024]{0:T(1024)S(1)}, f32[1024]{0:T(1024)S(1)}, f32[8,128]{1,0:T(8,128)}, f32[1024]{0:T(1024)S(1)}, /*index=5*/f32[8,128,32]{2...) while((s32[]{:T(128)}, f32[1024]{0:T(1024)S(1)}, f32[1024]{0:T(1024)S(1)}, ...), condition=%wide.region_19.20_spmd.clone, body=%wide.region_15.0_spmd.clone.sunk | while | flops 51393408 | bytes 1321588 | solution.py:58
  85.2 9.3 %while.336 = (s32[]{:T(128)}, f32[8,128]{1,0:T(8,128)S(1)}, f32[8,128]{1,0:T(8,128)S(1)}, f32[1024]{0:T(1024)S(1)}, f32[1024]{0:T(1024)S(1)}, /*index=5*/f32[8,1...) while((s32[]{:T(128)}, f32[8,128]{1,0:T(8,128)S(1)}, f32[8,128]{1,0:T(8,128)S(1)}, ...), condition=%wide.region_26.27_spmd, body=%wide.region_22.0_spmd.sunk | while | flops 51388032 | bytes 1274477 | solution.py:72
  94.5 10.4 %pmax.73 = f32[1024]{0:T(1024)S(1)} all-reduce(f32[1024]{0:T(1024)S(1)} %bitcast.904), channel_id=1, replica_groups=mesh['groups'=2,'row'=4,'col'=4] {'row'}, use_global_device_ids=true, to_apply=%region_27.28 | all-reduce | flops 1024 | bytes 8192 | tf_op jit(solution)/shard_map/pmax | solution.py:34
  104.9 8.4 %psum.150 = f32[1024]{0:T(1024)S(1)} all-reduce(f32[1024]{0:T(1024)S(1)} %bitcast_multiply_fusion.23), channel_id=1, replica_groups=mesh['groups'=2,'row'=4,'col'=4] {'row'}, use_global_device_ids=true, to_apply=%region_28.29 | all-reduce | flops 1024 | bytes 8192 | tf_op jit(solution)/shard_map/psum | solution.py:35
  133.2 9.3 %while.337 = (s32[]{:T(128)}, f32[8,128]{1,0:T(8,128)S(1)}, f32[8,128]{1,0:T(8,128)S(1)}, f32[1024]{0:T(1024)S(1)}, f32[1024]{0:T(1024)S(1)}, /*index=5*/f32[8,1...) while((s32[]{:T(128)}, f32[8,128]{1,0:T(8,128)S(1)}, f32[8,128]{1,0:T(8,128)S(1)}, ...), condition=%wide.region_40.41_spmd, body=%wide.region_36.40_spmd.sunk | while | flops 51388032 | bytes 1274477 | solution.py:72
  142.5 10.4 %pmax.75 = f32[1024]{0:T(1024)S(1)} all-reduce(f32[1024]{0:T(1024)S(1)} %bitcast.905), channel_id=1, replica_groups=mesh['groups'=2,'row'=4,'col'=4] {'row'}, use_global_device_ids=true, to_apply=%region_41.42 | all-reduce | flops 1024 | bytes 8192 | tf_op jit(solution)/shard_map/pmax | solution.py:34
  152.9 8.4 %psum.152 = f32[1024]{0:T(1024)S(1)} all-reduce(f32[1024]{0:T(1024)S(1)} %bitcast_multiply_fusion.22), channel_id=1, replica_groups=mesh['groups'=2,'row'=4,'col'=4] {'row'}, use_global_device_ids=true, to_apply=%region_42.43 | all-reduce | flops 1024 | bytes 8192 | tf_op jit(solution)/shard_map/psum | solution.py:35
  180.6 9.3 %while.338 = (s32[]{:T(128)}, f32[8,128]{1,0:T(8,128)S(1)}, f32[8,128]{1,0:T(8,128)S(1)}, f32[1024]{0:T(1024)S(1)}, f32[1024]{0:T(1024)S(1)}, /*index=5*/f32[8,1...) while((s32[]{:T(128)}, f32[8,128]{1,0:T(8,128)S(1)}, f32[8,128]{1,0:T(8,128)S(1)}, ...), condition=%wide.region_54.55_spmd, body=%wide.region_50.54_spmd.sunk | while | flops 51388032 | bytes 1274477 | solution.py:72
  190.0 10.4 %pmax.77 = f32[1024]{0:T(1024)S(1)} all-reduce(f32[1024]{0:T(1024)S(1)} %bitcast.906), channel_id=1, replica_groups=mesh['groups'=2,'row'=4,'col'=4] {'row'}, use_global_device_ids=true, to_apply=%region_55.56 | all-reduce | flops 1024 | bytes 8192 | tf_op jit(solution)/shard_map/pmax | solution.py:34
  200.4 8.4 %psum.154 = f32[1024]{0:T(1024)S(1)} all-reduce(f32[1024]{0:T(1024)S(1)} %bitcast_multiply_fusion.21), channel_id=1, replica_groups=mesh['groups'=2,'row'=4,'col'=4] {'row'}, use_global_device_ids=true, to_apply=%region_56.57 | all-reduce | flops 1024 | bytes 8192 | tf_op jit(solution)/shard_map/psum | solution.py:35
  228.7 9.3 %while.339 = (s32[]{:T(128)}, f32[8,128]{1,0:T(8,128)S(1)}, f32[8,128]{1,0:T(8,128)S(1)}, f32[1024]{0:T(1024)S(1)}, f32[1024]{0:T(1024)S(1)}, /*index=5*/f32[8,1...) while((s32[]{:T(128)}, f32[8,128]{1,0:T(8,128)S(1)}, f32[8,128]{1,0:T(8,128)S(1)}, ...), condition=%wide.region_68.69_spmd, body=%wide.region_64.68_spmd.sunk | while | flops 51388032 | bytes 1274477 | solution.py:72
  238.0 10.4 %pmax.79 = f32[1024]{0:T(1024)S(1)} all-reduce(f32[1024]{0:T(1024)S(1)} %bitcast.907), channel_id=1, replica_groups=mesh['groups'=2,'row'=4,'col'=4] {'row'}, use_global_device_ids=true, to_apply=%region_69.70 | all-reduce | flops 1024 | bytes 8192 | tf_op jit(solution)/shard_map/pmax | solution.py:34
  248.4 8.4 %psum.156 = f32[1024]{0:T(1024)S(1)} all-reduce(f32[1024]{0:T(1024)S(1)} %bitcast_multiply_fusion.20), channel_id=1, replica_groups=mesh['groups'=2,'row'=4,'col'=4] {'row'}, use_global_device_ids=true, to_apply=%region_70.71 | all-reduce | flops 1024 | bytes 8192 | tf_op jit(solution)/shard_map/psum | solution.py:35
  256.8 16.3 %while.345 = (s32[]{:T(128)}, f32[1024]{0:T(1024)S(1)}, f32[1024,32]{0,1:T(8,128)S(1)}, f32[8,128]{1,0:T(8,128)S(1)}, f32[8,128,32]{1,2,0:T(8,128)S(1)}, /*index...) while((s32[]{:T(128)}, f32[1024]{0:T(1024)S(1)}, ...), condition=%wide.region_75.76_spmd.clone, body=%wide.region_71.0_spmd.clone.sunk | while | flops 152249088 | bytes 2289816 | solution.py:110
  279.4 16.4 %while.346 = (s32[]{:T(128)}, f32[1024]{0:T(1024)S(1)}, f32[1024,32]{0,1:T(8,128)S(1)}, f32[8,128]{1,0:T(8,128)S(1)}, f32[8,128,32]{1,2,0:T(8,128)S(1)}, /*index...) while((s32[]{:T(128)}, f32[1024]{0:T(1024)S(1)}, ...), condition=%wide.region_81.82_spmd.clone, body=%wide.region_77.0_spmd.clone.sunk | while | flops 152250112 | bytes 2302112 | solution.py:110
  295.8 10.4 %psum.158 = f32[1024]{0:T(1024)S(1)} all-reduce(f32[1024]{0:T(1024)S(1)} %bitcast.908), channel_id=1, replica_groups=mesh['groups'=2,'row'=4,'col'=4] {'row'}, use_global_device_ids=true, to_apply=%region_82.83 | all-reduce | flops 1024 | bytes 8192 | tf_op jit(solution)/shard_map/psum | solution.py:169
  306.3 16.4 %while.347 = (s32[]{:T(128)}, f32[1024]{0:T(1024)S(1)}, f32[1024,32]{0,1:T(8,128)S(1)}, f32[8,128]{1,0:T(8,128)S(1)}, f32[8,128,32]{1,2,0:T(8,128)S(1)}, /*index...) while((s32[]{:T(128)}, f32[1024]{0:T(1024)S(1)}, ...), condition=%wide.region_87.88_spmd.clone, body=%wide.region_83.87_spmd.clone.sunk | while | flops 152249216 | bytes 2291360 | solution.py:110
  328.9 16.4 %while.348 = (s32[]{:T(128)}, f32[1024]{0:T(1024)S(1)}, f32[1024,32]{0,1:T(8,128)S(1)}, f32[8,128]{1,0:T(8,128)S(1)}, f32[8,128,32]{1,2,0:T(8,128)S(1)}, /*index...) while((s32[]{:T(128)}, f32[1024]{0:T(1024)S(1)}, ...), condition=%wide.region_93.94_spmd.clone, body=%wide.region_89.0_spmd.clone.sunk | while | flops 152250112 | bytes 2302112 | solution.py:110
  345.4 8.4 %psum.160 = f32[1024]{0:T(1024)S(1)} all-reduce(f32[1024]{0:T(1024)S(1)} %bitcast.909), channel_id=1, replica_groups=mesh['groups'=2,'row'=4,'col'=4] {'row'}, use_global_device_ids=true, to_apply=%region_94.95 | all-reduce | flops 1024 | bytes 8192 | tf_op jit(solution)/shard_map/psum | solution.py:169
  353.8 16.4 %while.349 = (s32[]{:T(128)}, f32[1024]{0:T(1024)S(1)}, f32[1024,32]{0,1:T(8,128)S(1)}, f32[8,128]{1,0:T(8,128)S(1)}, f32[8,128,32]{1,2,0:T(8,128)S(1)}, /*index...) while((s32[]{:T(128)}, f32[1024]{0:T(1024)S(1)}, ...), condition=%wide.region_99.100_spmd.clone, body=%wide.region_95.0_spmd.clone.sunk | while | flops 152249216 | bytes 2291360 | solution.py:110
  375.9 16.4 %while.350 = (s32[]{:T(128)}, f32[1024]{0:T(1024)S(1)}, f32[1024,32]{0,1:T(8,128)S(1)}, f32[8,128]{1,0:T(8,128)S(1)}, f32[8,128,32]{1,2,0:T(8,128)S(1)}, /*index...) while((s32[]{:T(128)}, f32[1024]{0:T(1024)S(1)}, ...), condition=%wide.region_105.106_spmd.clone, body=%wide.region_101.105_spmd.clone.sunk | while | flops 152250112 | bytes 2302112 | solution.py:110
  392.3 10.4 %psum.162 = f32[1024]{0:T(1024)S(1)} all-reduce(f32[1024]{0:T(1024)S(1)} %bitcast.910), channel_id=1, replica_groups=mesh['groups'=2,'row'=4,'col'=4] {'row'}, use_global_device_ids=true, to_apply=%region_106.107 | all-reduce | flops 1024 | bytes 8192 | tf_op jit(solution)/shard_map/psum | solution.py:169
  402.7 16.4 %while.351 = (s32[]{:T(128)}, f32[1024]{0:T(1024)S(1)}, f32[1024,32]{0,1:T(8,128)S(1)}, f32[8,128]{1,0:T(8,128)S(1)}, f32[8,128,32]{1,2,0:T(8,128)S(1)}, /*index...) while((s32[]{:T(128)}, f32[1024]{0:T(1024)S(1)}, ...), condition=%wide.region_111.112_spmd.clone, body=%wide.region_107.111_spmd.clone.sunk | while | flops 152249216 | bytes 2291360 | solution.py:110
  426.0 56.7 %while.352 = (s32[]{:T(128)}, f32[1024]{0:T(1024)}, f32[1024,32]{0,1:T(8,128)S(1)}, f32[8,128]{1,0:T(8,128)}, f32[8,128,32]{1,2,0:T(8,128)S(1)}, /*index=5*/f32[...) while((s32[]{:T(128)}, f32[1024]{0:T(1024)}, ...), condition=%wide.region_117.118_spmd.clone, body=%wide.region_113.117_spmd.clone.sunk | while | flops 152250112 | bytes 2416996 | solution.py:110
  482.7 8.4 %psum.164 = f32[1024]{0:T(1024)S(1)} all-reduce(f32[1024]{0:T(1024)} %bitcast.911), channel_id=1, replica_groups=mesh['groups'=2,'row'=4,'col'=4] {'row'}, use_global_device_ids=true, to_apply=%region_118.119 | all-reduce | flops 1024 | bytes 8192 | tf_op jit(solution)/shard_map/psum | solution.py:169
  491.7 47.1 %while.353 = (s32[]{:T(128)}, f32[1024]{0:T(1024)S(1)}, f32[1024,32]{0,1:T(8,128)S(1)}, f32[8,128]{1,0:T(8,128)}, f32[8,128,32]{1,2,0:T(8,128)S(1)}, /*index=5*/...) while((s32[]{:T(128)}, f32[1024]{0:T(1024)S(1)}, ...), condition=%wide.region_123.124_spmd.clone, body=%wide.region_119.0_spmd.clone.sunk | while | flops 152249216 | bytes 2373420 | solution.py:110
  545.0 54.7 %while.354 = (s32[]{:T(128)}, f32[1024]{0:T(1024)}, f32[1024,32]{0,1:T(8,128)S(1)}, f32[8,128]{1,0:T(8,128)}, f32[8,128,32]{1,2,0:T(8,128)S(1)}, /*index=5*/f32[...) while((s32[]{:T(128)}, f32[1024]{0:T(1024)}, ...), condition=%wide.region_129.130_spmd.clone, body=%wide.region_125.0_spmd.clone.sunk | while | flops 152119040 | bytes 2384700 | solution.py:110
  603.7 28.8 %all-reduce.3.cloned.1.call-done = f32[1024,32]{0,1:T(8,128)} async-done(((f32[1024,32]{0,1:T(8,128)}), f32[1024,32]{0,1:T(8,128)}) %all-reduce.3.cloned.1.call-update) | async-done | bytes 131088 | tf_op jit(solution)/shard_map/psum | solution.py:172
  633.9 35.5 %all-reduce.5.cloned.1.call-done = f32[1024,32]{0,1:T(8,128)} async-done(((f32[1024,32]{0,1:T(8,128)}), f32[1024,32]{0,1:T(8,128)}) %all-reduce.5.cloned.1.call-update) | async-done | bytes 131088 | tf_op jit(solution)/shard_map/psum | solution.py:175
  (1534 shorter events, 487.8 us)
Async XLA Ops:
  7.2 625.3 %all-reduce.3.cloned.1.call-start = ((), (), s32[]{:S(2)}) async-start(), calls=%async_computation | async-start | bytes 262144 | tf_op jit(solution)/shard_map/psum | solution.py:172
  39.6 12.1 %copy-start.44 = (f32[1024]{0:T(1024)}, f32[1024]{0:T(1024)S(1)}, u32[]{:S(2)}) copy-start(f32[1024]{0:T(1024)S(1)} %get-tuple-element.4855) | copy-start | bytes 12292
  273.7 5.6 copy-start.6
  295.8 10.4 %copy-start.13 = (f32[1024]{0:T(1024)}, f32[1024]{0:T(1024)S(1)}, u32[]{:S(2)}) copy-start(f32[1024]{0:T(1024)S(1)} %get-tuple-element.2010) | copy-start | bytes 12292
  295.8 10.4 %copy-start.19 = (f32[8,128]{1,0:T(8,128)}, f32[8,128]{1,0:T(8,128)S(1)}, u32[]{:S(2)}) copy-start(f32[8,128]{1,0:T(8,128)S(1)} %get-tuple-element.2011) | copy-start | bytes 12292
  345.3 8.4 %copy-start.21 = (f32[8,128]{1,0:T(8,128)}, f32[8,128]{1,0:T(8,128)S(1)}, u32[]{:S(2)}) copy-start(f32[8,128]{1,0:T(8,128)S(1)} %get-tuple-element.2014) | copy-start | bytes 12292
  345.3 8.4 %copy-start.12 = (f32[1024]{0:T(1024)}, f32[1024]{0:T(1024)S(1)}, u32[]{:S(2)}) copy-start(f32[1024]{0:T(1024)S(1)} %get-tuple-element.2013) | copy-start | bytes 12292
  370.2 5.7 copy-start.31
  392.3 10.4 %copy-start.23 = (f32[8,128]{1,0:T(8,128)}, f32[8,128]{1,0:T(8,128)S(1)}, u32[]{:S(2)}) copy-start(f32[8,128]{1,0:T(8,128)S(1)} %get-tuple-element.2017) | copy-start | bytes 12292
  392.3 10.4 %copy-start.11 = (f32[1024]{0:T(1024)}, f32[1024]{0:T(1024)S(1)}, u32[]{:S(2)}) copy-start(f32[1024]{0:T(1024)S(1)} %get-tuple-element.2016) | copy-start | bytes 12292
  419.2 5.7 copy-start.33
  431.1 1.3 copy-start.16
  431.1 1.3 copy-start.8
  438.2 1.3 copy-start.16
  438.2 1.3 copy-start.8
  445.3 1.3 copy-start.16
  452.4 1.3 copy-start.16
  452.4 1.3 copy-start.8
  459.4 1.3 copy-start.16
  459.4 1.3 copy-start.8
  466.5 1.3 copy-start.16
  466.5 1.3 copy-start.8
  473.6 1.3 copy-start.16
  473.6 1.3 copy-start.8
  480.7 1.3 copy-start.16
  480.7 1.3 copy-start.8
  482.7 8.4 %copy-start.41 = (f32[1024]{0:T(1024)}, f32[1024]{0:T(1024)S(1)}, u32[]{:S(2)}) copy-start(f32[1024]{0:T(1024)S(1)} %get-tuple-element.4853) | copy-start | bytes 12292
  482.7 9.0 %copy-start.2 = (f32[8,128,32]{1,2,0:T(8,128)}, f32[8,128,32]{1,2,0:T(8,128)S(1)}, u32[]{:S(2)}) copy-start(f32[8,128,32]{1,2,0:T(8,128)S(1)} %get-tuple-element.2046) | copy-start | bytes 393220
  538.8 6.3 copy-start.4
  601.3 1.5 copy-start.3
  601.3 1.5 copy-start.5
  602.0 67.4 %all-reduce.5.cloned.1.call-start = ((), (), s32[]{:S(2)}) async-start(), calls=%async_computation.1 | async-start | bytes 262144 | tf_op jit(solution)/shard_map/psum | solution.py:175
  (145 other events, 107.7 us)
Sparse Core Ops, SparseCore 0:
  602.2 30.2 all-reduce.2
  634.9 34.4 all-reduce.4
where the time goes:
time: 683 us; the launch traced here: 678 us
  blocking collectives  223 us (33%)
  matrix products  221 us (32%)
  local copies, waits for them, and re-layouts  90.5 us (13%)
  waiting for transfers between devices  64.3 us (9%)
  other arithmetic  56.1 us (8%)
  between operations  14.9 us (2%)
  loops' own time  7.66 us (1%)
    dot_general x160, matrix products, pair_cost(): lax.dot_general(row_pts, col_pts, (((1,), (1,)), ((), ())), precision=HIG...  140 us
    pmax x5, blocking collectives, reduce_lse(): highest = lax.pmax(maxima, 'row')  53.6 us
    dot_general x80, matrix products, adjoint_advance(): lax.dot_general(weights, x_local, (((0,), (0,)), ((), ())), precision=HIG...  47.8 us
    psum x5, blocking collectives, reduce_lse(): totals = lax.psum(totals * jnp.exp(maxima - highest), 'row')  41.9 us
    psum x4, blocking collectives, on_device(): adj_cols = -lax.psum(col_part, 'row')  37.5 us
    psum x1, waiting for transfers between devices, on_device(): whole_y = lax.psum(part_y, 'row')  35.5 us
    dynamic_update_slice x160, local copies, waits for them, and re-layouts, col_update(): lax.scan(col_advance, jnp.float32(0.0), split_blocks(y_local, width))  35.5 us
    while x328, local copies, waits for them, and re-layouts  34.8 us
  transfers between devices with their start and end apart: 2, of which 2 were waited for; matrix products, arithmetic and copies ran while one was open for 0% of the time, Pallas kernels for 0%

commit v1 on v0

v1 whole, which is shorter than its diff:
```python
import functools
import math

import jax
import jax.numpy as jnp
from jax import lax
from jax.experimental import pallas as pl
from jax.experimental.pallas import tpu as pltpu
from jax.sharding import PartitionSpec as P

ITERS = 5
EPSILON = 0.05
SCALE = 1.0 / (EPSILON * math.log(2.0))
DEPTH = 256
CHUNK = 256
F32 = jnp.float32
BF16 = jnp.bfloat16
VMEM_LIMIT = 48 * 1024 * 1024


def split3(v):
    high = v.astype(BF16).astype(F32)
    rest = v - high
    mid = rest.astype(BF16).astype(F32)
    low = (rest - mid).astype(BF16).astype(F32)
    return high, mid, low


def vmem(count):
    return [pl.BlockSpec(memory_space=pltpu.VMEM)] * count


def call(body, outs, count, scratch=()):
    return pl.pallas_call(
        body,
        out_shape=outs,
        in_specs=vmem(count),
        out_specs=vmem(len(outs)),
        scratch_shapes=list(scratch),
        compiler_params=pltpu.CompilerParams(vmem_limit_bytes=VMEM_LIMIT),
    )


def shape(dims, dtype=F32):
    return jax.ShapeDtypeStruct(dims, dtype)


def factors(points, order):
    parts = split3(points)
    width = points.shape[1]
    blocks = [parts[o] for o in order]
    zero16 = jnp.zeros((16, width), F32)
    tail = jnp.zeros((DEPTH - 144 - 2 * points.shape[0], width), F32)
    return jnp.concatenate(blocks[:4] + [zero16] + blocks[4:] + [tail], axis=0)


X_ORDER = (0, 0, 1, 0, 2, 1)
Y_ORDER = (0, 1, 0, 2, 0, 1)


def prepare_body(x_ref, y_ref, ax0, ax1, ay0, ay1, bx, by, start_ref):
    x = x_ref[...]
    y = y_ref[...]
    xf = factors(x * (2.0 * SCALE), X_ORDER)
    yf = factors(y, Y_ORDER)
    for factor, left0, left1, right in ((xf, ax0, ax1, bx), (yf, ay0, ay1, by)):
        right[...] = factor.astype(BF16)
        turned = factor.T
        left0[...] = turned[:, :128].astype(BF16)
        left1[...] = turned[:, 128:]
    start_ref[...] = -SCALE * jnp.sum(y * y, axis=0, keepdims=True)


def left_factor(left0, left1, pot, adj=None):
    width = pot.shape[1]
    high, mid, low = split3(pot)
    one = jnp.ones((1, width), F32)
    rows = [high, mid, low, one, one, one, jnp.zeros_like(one)]
    rows.append(jnp.zeros_like(one) if adj is None else adj)
    rows.append(jnp.zeros((120, width), F32))
    turned = jnp.concatenate(rows, axis=0).T
    column = None
    if adj is not None:
        column = turned[:, 7:8]
        lane = lax.broadcasted_iota(jnp.int32, turned.shape, 1)
        turned = jnp.where(lane == 7, 0.0, turned)
    return jnp.concatenate([left0[...], (left1[...] + turned).astype(BF16)], axis=1), column


def right_rows(pot):
    width = pot.shape[1]
    one = jnp.ones((3, width), F32)
    high, mid, low = split3(pot)
    return jnp.concatenate([one, high, mid, low, jnp.zeros((10, width), F32)], axis=0).astype(BF16)


def right_chunk(right, rows, at, wide):
    return jnp.concatenate(
        [right[0:128, at : at + wide], rows[:, at : at + wide], right[144:DEPTH, at : at + wide]], axis=0
    )


def matmul(a, b):
    return jnp.dot(a, b, preferred_element_type=F32)


def partial_lse(left, right, out):
    width = right.shape[1]
    rows = right_rows(jnp.zeros((1, width), F32))
    wide = min(CHUNK, width)
    for at in range(0, width, wide):
        scores = matmul(left, right_chunk(right, rows, at, wide))
        top = jnp.max(scores, axis=0, keepdims=True)
        out[0:1, at : at + wide] = top
        out[1:2, at : at + wide] = jnp.sum(jnp.exp2(scores - top), axis=0, keepdims=True)


def join_lse(parts, log_mass):
    tops = [p[0:1, :] for p in parts]
    top = functools.reduce(jnp.maximum, tops)
    total = sum(p[1:2, :] * jnp.exp2(t - top) for p, t in zip(parts, tops))
    return log_mass - (top + jnp.log2(total))


def first_body(left0, left1, right, pot, out):
    left, unused = left_factor(left0, left1, pot[...])
    partial_lse(left, right, out)


def forward_body(log_mass, *refs):
    left0, left1, right = refs[:3]
    parts, (pot_out, out) = refs[3:-2], refs[-2:]
    pot = join_lse([p[...] for p in parts], log_mass)
    pot_out[...] = pot
    left, unused = left_factor(left0, left1, pot)
    partial_lse(left, right, out)


def weighted_sums(left, column, right, rows, out):
    width = right.shape[1]
    wide = min(CHUNK, width)
    for at in range(0, width, wide):
        scores = matmul(left, right_chunk(right, rows, at, wide))
        out[:, at : at + wide] = jnp.sum(jnp.exp2(scores) * column, axis=0, keepdims=True)


def turn_body(log_mass, log_scale, left0, left1, right, pot_right, *refs):
    parts, (pot_out, out) = refs[:-2], refs[-2:]
    pot = join_lse([p[...] for p in parts], log_mass)
    pot_out[...] = pot
    left, column = left_factor(left0, left1, pot, jnp.ones_like(pot))
    weighted_sums(left, column, right, right_rows(pot_right[...] + log_scale), out)


def backward_body(leading, log_scale, left0, left1, right, pot_left, pot_right, *refs):
    parts, (adj_out, out) = refs[:-2], refs[-2:]
    adj = leading - sum(p[...] for p in parts)
    adj_out[...] = adj
    left, column = left_factor(left0, left1, pot_left[...], adj)
    weighted_sums(left, column, right, right_rows(pot_right[...] + log_scale), out)


def gradient_body(dim, log_cols, log_rows, col_axis, row_axis, ax0, ax1, by, x_ref, y_ref, *refs):
    pots_rows = refs[:ITERS]
    pots_cols = refs[ITERS : 2 * ITERS + 1]
    adjs_rows = refs[2 * ITERS + 1 : 3 * ITERS + 1]
    adjs_cols = refs[3 * ITERS + 1 : 4 * ITERS + 1]
    n_col = lax.axis_size(col_axis)
    n_row = lax.axis_size(row_axis)
    outs = refs[4 * ITERS + 1 :]
    outs_x, outs_y = outs[:n_col], outs[n_col : n_col + n_row]
    cols_rows, x_parts, y_parts, gx, gy = outs[n_col + n_row :]
    count_rows, count_cols = x_ref.shape[1], y_ref.shape[1]

    stack = [p[...] + log_cols for p in pots_rows] + [a[...] for a in adjs_rows]
    stack.append(jnp.zeros((128 - len(stack), count_rows), F32))
    cols_rows[...] = jnp.concatenate(stack, axis=0).T

    x = x_ref[...]
    y = y_ref[...]
    one = jnp.ones((1, count_cols), F32)
    pad = jnp.zeros((31, count_cols), F32)
    y_parts[...] = jnp.concatenate(list(split3(y)) + [one, pad], axis=0).T.astype(BF16)
    one = jnp.ones((1, count_rows), F32)
    pad = jnp.zeros((31, count_rows), F32)
    x_parts[...] = jnp.concatenate(list(split3(x)) + [one, pad], axis=0).astype(BF16)
    gy[...] = jnp.zeros_like(gy)

    high = 128

    def block(step, carry):
        at = pl.ds(pl.multiple_of(step * high, high), high)
        left = jnp.concatenate([ax0[at, :], ax1[at, :].astype(BF16)], axis=1)
        inner = matmul(left, by[...])
        columns = cols_rows[at, :]
        total = jnp.zeros_like(inner)
        for k in range(ITERS):
            base = inner + columns[:, k : k + 1]
            total += jnp.exp2(base + pots_cols[k + 1][...]) * adjs_cols[k][...]
            total += jnp.exp2(base + (pots_cols[k][...] + (log_rows - log_cols))) * columns[:, ITERS + k : ITERS + k + 1]
        upper = total.astype(BF16)
        lower = (total - upper.astype(F32)).astype(BF16)
        gx[at, :] = matmul(upper, y_parts[...]) + matmul(lower, y_parts[...])
        gy[...] += matmul(x_parts[:, at], upper) + matmul(x_parts[:, at], lower)
        return carry

    lax.fori_loop(0, count_rows // high, block, 0)

    def finish(points, sums):
        mixed = sums[0:dim] + sums[dim : 2 * dim] + sums[2 * dim : 3 * dim]
        return 2.0 * (points * sums[3 * dim : 3 * dim + 1] - mixed)

    for value, outs_, count, axis, held in (
        (finish(x, gx[...].T), outs_x, n_col, col_axis, gx),
        (finish(y, gy[...]), outs_y, n_row, row_axis, gy),
    ):
        share = value.shape[1] // count
        pieces = [value[:, p * share : (p + 1) * share] for p in range(count)]
        me = lax.axis_index(axis)
        for s in range(count):
            target = lax.rem(me + s, count)
            chosen = pieces[0]
            for p in range(1, count):
                chosen = jnp.where(target == p, pieces[p], chosen)
            outs_[s][...] = chosen


def exchange(value, axis):
    size = lax.axis_size(axis)
    return [value] + [
        lax.ppermute(value, axis, [(d, (d + s) % size) for d in range(size)]) for s in range(1, size)
    ]


def scatter(pieces, axis):
    size = lax.axis_size(axis)
    got = [pieces[0]] + [
        lax.ppermute(pieces[s], axis, [(d, (d + s) % size) for d in range(size)]) for s in range(1, size)
    ]
    return sum(got[1:], got[0])


def on_device(x_points, y_points):
    x = x_points.T
    y = y_points.T
    dim, count_rows = x.shape
    count_cols = y.shape[1]
    n_row, n_col = lax.axis_size("row"), lax.axis_size("col")
    log_rows = math.log2(count_rows * n_row)
    log_cols = math.log2(count_cols * n_col)
    row, col = (1, count_rows), (1, count_cols)

    ax0, ax1, ay0, ay1, bx, by, start = call(
        prepare_body,
        [
            shape((count_rows, 128), BF16),
            shape((count_rows, 128)),
            shape((count_cols, 128), BF16),
            shape((count_cols, 128)),
            shape((DEPTH, count_rows), BF16),
            shape((DEPTH, count_cols), BF16),
            shape(col),
        ],
        2,
    )(x, y)

    pots_rows, pots_cols = [], [start]
    (part,) = call(first_body, [shape((2, count_rows))], 4)(ay0, ay1, bx, start)
    for k in range(ITERS):
        got = exchange(part, "col")
        pot, part = call(
            functools.partial(forward_body, -log_rows), [shape(row), shape((2, count_cols))], 3 + n_col
        )(ax0, ax1, by, *got)
        pots_rows.append(pot)
        got = exchange(part, "row")
        if k < ITERS - 1:
            pot, part = call(
                functools.partial(forward_body, -log_cols), [shape(col), shape((2, count_rows))], 3 + n_row
            )(ay0, ay1, bx, *got)
            pots_cols.append(pot)
    pot, part = call(
        functools.partial(turn_body, -log_cols, log_cols), [shape(col), shape(row)], 4 + n_row
    )(ay0, ay1, bx, pots_rows[-1], *got)
    pots_cols.append(pot)

    adjs_rows, adjs_cols = [None] * ITERS, [None] * ITERS
    adjs_cols[-1] = jnp.ones(col, F32)
    for k in reversed(range(ITERS)):
        leading = 1.0 if k == ITERS - 1 else 0.0
        got = exchange(part, "col")
        if k == 0:
            break
        adjs_rows[k], part = call(
            functools.partial(backward_body, leading, log_rows), [shape(row), shape(col)], 5 + n_col
        )(ax0, ax1, by, pots_rows[k], pots_cols[k], *got)
        got = exchange(part, "row")
        adjs_cols[k - 1], part = call(
            functools.partial(backward_body, 0.0, log_cols), [shape(col), shape(row)], 5 + n_row
        )(ay0, ay1, bx, pots_cols[k], pots_rows[k - 1], *got)
    adjs_rows[0] = -sum(got[1:], got[0]) if ITERS > 1 else 1.0 - sum(got[1:], got[0])

    share_x, share_y = count_rows // n_col, count_cols // n_row
    outs = call(
        functools.partial(gradient_body, dim, log_cols, log_rows, "col", "row"),
        [shape((dim, share_x))] * n_col + [shape((dim, share_y))] * n_row,
        5 + 4 * ITERS + 1,
        [
            pltpu.VMEM((count_rows, 128), F32),
            pltpu.VMEM((128, count_rows), BF16),
            pltpu.VMEM((count_cols, 128), BF16),
            pltpu.VMEM((count_rows, 128), F32),
            pltpu.VMEM((128, count_cols), F32),
        ],
    )(ax0, ax1, by, x, y, *pots_rows, *pots_cols, *adjs_rows, *adjs_cols)
    grad_x = scatter(outs[:n_col], "col")
    grad_y = scatter(outs[n_col:], "row")
    return (grad_x.T, grad_y.T)


def solution(mesh):
    in_specs = (P(("groups", "row"), None), P(("groups", "col"), None))
    out_specs = (P(("groups", "row", "col"), None), P(("groups", "col", "row"), None))
    return jax.shard_map(
        on_device, mesh=mesh, in_specs=in_specs, out_specs=out_specs, check_vma=False
    )
```

time: 683 us -> 153 us (0.22)
  blocking collectives: 223 us -> 0 us
  matrix products: 221 us -> 0 us
  local copies, waits for them, and re-layouts: 90.5 us -> 1.81 us
  starting transfers between devices: 0.08 us -> 68.4 us
  other arithmetic: 56.1 us -> 1.26 us
  Pallas kernels: 0 us -> 35.4 us
  waiting for transfers between devices: 64.3 us -> 44.6 us
  between operations: 14.9 us -> 0.88 us
  loops' own time: 7.66 us -> 0 us
    dot_general x320 -> x0, matrix products: 221 us -> none  [the longest x160 140 us: pair_cost(): lax.dot_general(row_pts, col_pts, (((1,), (1,)), ((), ())), precision=HIG...]
    psum x19 -> x0, blocking collectives: 139 us -> none  [the longest x5 41.9 us: reduce_lse(): totals = lax.psum(totals * jnp.exp(maxima - highest), 'row')]
    pmax x10 -> x0, blocking collectives: 84.8 us -> none  [the longest x5 53.6 us: reduce_lse(): highest = lax.pmax(maxima, 'row')]
    ppermute x0 -> x63, starting transfers between devices: none -> 68.4 us  [the longest x57 63.6 us: exchange(): lax.ppermute(value, axis, [(d, (d + s) % size) for d in range(size)])]
    psum x2 -> x0, waiting for transfers between devices: 64.3 us -> none  [the longest x1 35.5 us: on_device(): whole_y = lax.psum(part_y, 'row')]
    ppermute x0 -> x63, waiting for transfers between devices: none -> 44.6 us  [the longest x57 40.1 us: exchange(): lax.ppermute(value, axis, [(d, (d + s) % size) for d in range(size)])]
    dynamic_update_slice x160 -> x0, local copies, waits for them, and re-layouts: 35.5 us -> none  [col_update(): lax.scan(col_advance, jnp.float32(0.0), split_blocks(y_local, width))]
    pallas_call x0 -> x21, Pallas kernels: none -> 35.4 us  [the longest x1 13.4 us: on_device(): call(functools.partial(gradient_body, dim, log_cols, log_rows, 'col', 'ro...]
  transfers between devices with their start and end apart: 2 -> 63, of which waited for: 2 -> 54; matrix products, arithmetic and copies ran while one was open for 0% -> 0% of each run, Pallas kernels for 0% -> 0%
where the time goes in v1:
time: 153 us; the launch traced here: 152 us
  starting transfers between devices  68.4 us (45%)
  waiting for transfers between devices  44.6 us (29%)
  Pallas kernels  35.4 us (23%)
  local copies, waits for them, and re-layouts  1.81 us (1%)
    ppermute x57, starting transfers between devices, exchange(): lax.ppermute(value, axis, [(d, (d + s) % size) for d in range(size)])  63.6 us
    ppermute x57, waiting for transfers between devices, exchange(): lax.ppermute(value, axis, [(d, (d + s) % size) for d in range(size)])  40.1 us
    pallas_call x1, Pallas kernels, on_device(): call(functools.partial(gradient_body, dim, log_cols, log_rows, 'col', 'ro...  13.4 us
    pallas_call x5, Pallas kernels, on_device(): call(functools.partial(forward_body, -log_rows), [shape(row), shape((2, c...  6.78 us
    pallas_call x4, Pallas kernels, on_device(): call(functools.partial(forward_body, -log_cols), [shape(col), shape((2, c...  5.42 us
    ppermute x6, starting transfers between devices, scatter(): lax.ppermute(pieces[s], axis, [(d, (d + s) % size) for d in range(size)])  4.77 us
    ppermute x6, waiting for transfers between devices, scatter(): lax.ppermute(pieces[s], axis, [(d, (d + s) % size) for d in range(size)])  4.55 us
    pallas_call x4, Pallas kernels, on_device(): call(functools.partial(backward_body, leading, log_rows), [shape(row), sh...  3.6 us
  transfers between devices with their start and end apart: 63, of which 54 were waited for; matrix products, arithmetic and copies ran while one was open for 0% of the time, Pallas kernels for 0%

profile of v1, /device:TPU:0, one launch (start us, length us, event | category | flops | bytes accessed | tf_op | source)
XLA Modules:
  0.0 152.4 jit_solution(4665390418076779405)
XLA Ops:
  4.6 2.6 %collective-permute-start.1 = (f32[2,1024]{1,0:T(2,128)S(1)}, f32[2,1024]{1,0:T(2,128)S(1)}, u32[]{:S(2)}, u32[]{:S(2)}) collective-permute-start(f32[2,1024]{1,0:T(2,128)S(1)} %shard_map.42.refs_3_), channel_id=1, source_target_pairs={{0,2},{1,3},{2,0},{3,1},{4,6},{5,7},{6,4},{7,5},{8,10},{9,11},{10,... | collective-permute-start | bytes 24584 | tf_op jit(solution)/shard_map/ppermute | solution.py:231
  7.2 1.4 collective-permute-start.2
  11.3 1.6 %collective-permute-start.3 = (f32[2,1024]{1,0:T(2,128)S(1)}, f32[2,1024]{1,0:T(2,128)S(1)}, u32[]{:S(2)}, u32[]{:S(2)}) collective-permute-start(f32[2,1024]{1,0:T(2,128)S(1)} %get-tuple-element.61.refs_3_), channel_id=1, source_target_pairs={{0,4},{4,8},{8,12},{12,0},{1,5},{5,9},{9,13},{13,1},{2,6},{6,10},{... | collective-permute-start | bytes 24584 | tf_op jit(solution)/shard_map/ppermute | solution.py:231
  12.9 2.6 %collective-permute-start.4 = (f32[2,1024]{1,0:T(2,128)S(1)}, f32[2,1024]{1,0:T(2,128)S(1)}, u32[]{:S(2)}, u32[]{:S(2)}) collective-permute-start(f32[2,1024]{1,0:T(2,128)S(1)} %get-tuple-element.61.refs_3_), channel_id=1, source_target_pairs={{0,8},{4,12},{8,0},{12,4},{1,9},{5,13},{9,1},{13,5},{2,10},{6,14},... | collective-permute-start | bytes 24584 | tf_op jit(solution)/shard_map/ppermute | solution.py:231
  17.5 1.7 %collective-permute-done.5.refs_6_ = f32[2,1024]{1,0:T(2,128)S(1)} collective-permute-done((f32[2,1024]{1,0:T(2,128)S(1)}, f32[2,1024]{1,0:T(2,128)S(1)}, u32[]{:S(2)}, u32[]{:S(2)}) %collective-permute-start.5) | collective-permute-done | bytes 8224 | tf_op jit(solution)/shard_map/ppermute | solution.py:231
  21.6 1.4 collective-permute-start.8
  26.0 3.5 %collective-permute-start.10 = (f32[2,1024]{1,0:T(2,128)S(1)}, f32[2,1024]{1,0:T(2,128)S(1)}, u32[]{:S(2)}, u32[]{:S(2)}) collective-permute-start(f32[2,1024]{1,0:T(2,128)S(1)} %get-tuple-element.64.refs_3_), channel_id=1, source_target_pairs={{0,8},{4,12},{8,0},{12,4},{1,9},{5,13},{9,1},{13,5},{2,10},{6,14},... | collective-permute-start | bytes 24584 | tf_op jit(solution)/shard_map/ppermute | solution.py:231
  29.6 1.6 %collective-permute-done.9.refs_4_ = f32[2,1024]{1,0:T(2,128)S(1)} collective-permute-done((f32[2,1024]{1,0:T(2,128)S(1)}, f32[2,1024]{1,0:T(2,128)S(1)}, u32[]{:S(2)}, u32[]{:S(2)}) %collective-permute-start.9) | collective-permute-done | bytes 8224 | tf_op jit(solution)/shard_map/ppermute | solution.py:231
  31.2 1.9 %collective-permute-done.11.refs_6_ = f32[2,1024]{1,0:T(2,128)S(1)} collective-permute-done((f32[2,1024]{1,0:T(2,128)S(1)}, f32[2,1024]{1,0:T(2,128)S(1)}, u32[]{:S(2)}, u32[]{:S(2)}) %collective-permute-start.11) | collective-permute-done | bytes 8224 | tf_op jit(solution)/shard_map/ppermute | solution.py:231
  35.7 1.4 collective-permute-start.14
  40.5 1.8 %collective-permute-start.16 = (f32[2,1024]{1,0:T(2,128)S(1)}, f32[2,1024]{1,0:T(2,128)S(1)}, u32[]{:S(2)}, u32[]{:S(2)}) collective-permute-start(f32[2,1024]{1,0:T(2,128)S(1)} %get-tuple-element.67.refs_3_), channel_id=1, source_target_pairs={{0,8},{4,12},{8,0},{12,4},{1,9},{5,13},{9,1},{13,5},{2,10},{6,14},... | collective-permute-start | bytes 24584 | tf_op jit(solution)/shard_map/ppermute | solution.py:231
  43.7 1.6 %collective-permute-done.15.refs_4_ = f32[2,1024]{1,0:T(2,128)S(1)} collective-permute-done((f32[2,1024]{1,0:T(2,128)S(1)}, f32[2,1024]{1,0:T(2,128)S(1)}, u32[]{:S(2)}, u32[]{:S(2)}) %collective-permute-start.15) | collective-permute-done | bytes 8224 | tf_op jit(solution)/shard_map/ppermute | solution.py:231
  48.5 1.4 collective-permute-start.20
  52.6 1.9 %collective-permute-start.21 = (f32[2,1024]{1,0:T(2,128)S(1)}, f32[2,1024]{1,0:T(2,128)S(1)}, u32[]{:S(2)}, u32[]{:S(2)}) collective-permute-start(f32[2,1024]{1,0:T(2,128)S(1)} %get-tuple-element.70.refs_3_), channel_id=1, source_target_pairs={{0,4},{4,8},{8,12},{12,0},{1,5},{5,9},{9,13},{13,1},{2,6},{6,10},{... | collective-permute-start | bytes 24584 | tf_op jit(solution)/shard_map/ppermute | solution.py:231
  54.5 1.9 %collective-permute-start.22 = (f32[2,1024]{1,0:T(2,128)S(1)}, f32[2,1024]{1,0:T(2,128)S(1)}, u32[]{:S(2)}, u32[]{:S(2)}) collective-permute-start(f32[2,1024]{1,0:T(2,128)S(1)} %get-tuple-element.70.refs_3_), channel_id=1, source_target_pairs={{0,8},{4,12},{8,0},{12,4},{1,9},{5,13},{9,1},{13,5},{2,10},{6,14},... | collective-permute-start | bytes 24584 | tf_op jit(solution)/shard_map/ppermute | solution.py:231
  62.5 1.4 collective-permute-start.26
  67.4 2.3 %collective-permute-start.28 = (f32[2,1024]{1,0:T(2,128)S(1)}, f32[2,1024]{1,0:T(2,128)S(1)}, u32[]{:S(2)}, u32[]{:S(2)}) collective-permute-start(f32[2,1024]{1,0:T(2,128)S(1)} %get-tuple-element.77.refs_0_), channel_id=1, source_target_pairs={{0,8},{4,12},{8,0},{12,4},{1,9},{5,13},{9,1},{13,5},{2,10},{6,14},... | collective-permute-start | bytes 24584 | tf_op jit(solution)/shard_map/ppermute | solution.py:231
  70.7 1.4 collective-permute-done.27.refs_1_
  75.4 1.4 collective-permute-start.32
  79.0 1.5 collective-permute-start.33
  80.5 2.0 %collective-permute-start.34 = (f32[1,1024]{1,0:T(1,128)S(1)}, f32[1,1024]{1,0:T(1,128)S(1)}, u32[]{:S(2)}, u32[]{:S(2)}) collective-permute-start(f32[1,1024]{1,0:T(1,128)S(1)} %get-tuple-element.80.refs_0_), channel_id=1, source_target_pairs={{0,8},{4,12},{8,0},{12,4},{1,9},{5,13},{9,1},{13,5},{2,10},{6,14},... | collective-permute-start | bytes 12296 | tf_op jit(solution)/shard_map/ppermute | solution.py:231
  82.9 1.5 collective-permute-done.33.refs_1_
  92.8 1.8 %collective-permute-start.40 = (f32[1,1024]{1,0:T(1,128)S(1)}, f32[1,1024]{1,0:T(1,128)S(1)}, u32[]{:S(2)}, u32[]{:S(2)}) collective-permute-start(f32[1,1024]{1,0:T(1,128)S(1)} %get-tuple-element.82.refs_0_), channel_id=1, source_target_pairs={{0,8},{4,12},{8,0},{12,4},{1,9},{5,13},{9,1},{13,5},{2,10},{6,14},... | collective-permute-start | bytes 12296 | tf_op jit(solution)/shard_map/ppermute | solution.py:231
  95.7 1.6 %collective-permute-done.39.refs_1_ = f32[1,1024]{1,0:T(1,128)S(1)} collective-permute-done((f32[1,1024]{1,0:T(1,128)S(1)}, f32[1,1024]{1,0:T(1,128)S(1)}, u32[]{:S(2)}, u32[]{:S(2)}) %collective-permute-start.39) | collective-permute-done | bytes 4128 | tf_op jit(solution)/shard_map/ppermute | solution.py:231
  103.9 1.6 %collective-permute-start.45 = (f32[1,1024]{1,0:T(1,128)S(1)}, f32[1,1024]{1,0:T(1,128)S(1)}, u32[]{:S(2)}, u32[]{:S(2)}) collective-permute-start(f32[1,1024]{1,0:T(1,128)S(1)} %get-tuple-element.84.refs_0_), channel_id=1, source_target_pairs={{0,4},{4,8},{8,12},{12,0},{1,5},{5,9},{9,13},{13,1},{2,6},{6,10},{... | collective-permute-start | bytes 12296 | tf_op jit(solution)/shard_map/ppermute | solution.py:231
  105.5 1.9 %collective-permute-start.46 = (f32[1,1024]{1,0:T(1,128)S(1)}, f32[1,1024]{1,0:T(1,128)S(1)}, u32[]{:S(2)}, u32[]{:S(2)}) collective-permute-start(f32[1,1024]{1,0:T(1,128)S(1)} %get-tuple-element.84.refs_0_), channel_id=1, source_target_pairs={{0,8},{4,12},{8,0},{12,4},{1,9},{5,13},{9,1},{13,5},{2,10},{6,14},... | collective-permute-start | bytes 12296 | tf_op jit(solution)/shard_map/ppermute | solution.py:231
  108.0 1.4 collective-permute-done.45.refs_1_
  117.7 2.0 %collective-permute-start.52 = (f32[1,1024]{1,0:T(1,128)S(1)}, f32[1,1024]{1,0:T(1,128)S(1)}, u32[]{:S(2)}, u32[]{:S(2)}) collective-permute-start(f32[1,1024]{1,0:T(1,128)S(1)} %get-tuple-element.86.refs_0_), channel_id=1, source_target_pairs={{0,8},{4,12},{8,0},{12,4},{1,9},{5,13},{9,1},{13,5},{2,10},{6,14},... | collective-permute-start | bytes 12296 | tf_op jit(solution)/shard_map/ppermute | solution.py:231
  125.6 2.4 %collective-permute-done.55 = f32[1,1024]{1,0:T(1,128)S(1)} collective-permute-done((f32[1,1024]{1,0:T(1,128)S(1)}, f32[1,1024]{1,0:T(1,128)S(1)}, u32[]{:S(2)}, u32[]{:S(2)}) %collective-permute-start.55) | collective-permute-done | bytes 4128 | tf_op jit(solution)/shard_map/ppermute | solution.py:231
  128.4 13.4 %shard_map.61 = (f32[32,256]{1,0:T(8,128)S(1)}, f32[32,256]{1,0:T(8,128)S(1)}, f32[32,256]{1,0:T(8,128)S(1)}, f32[32,256]{1,0:T(8,128)S(1)}, f32[32,256]{1,0:T(8...) custom-call(bf16[1024,128]{1,0:T(8,128)(2,1)S(1)} %get-tuple-element.53.refs_0_.left0.ax0, ...), custom_call_target="tpu_custom_call" | custom-call | tf_op jit(solution)/shard_map/pallas_call | solution.py:303
  143.1 2.9 %collective-permute-start.62 = (f32[32,256]{1,0:T(8,128)S(1)}, f32[32,256]{1,0:T(8,128)S(1)}, u32[]{:S(2)}, u32[]{:S(2)}) collective-permute-start(f32[32,256]{1,0:T(8,128)S(1)} %get-tuple-element.103), channel_id=1, source_target_pairs={{0,12},{4,0},{8,4},{12,8},{1,13},{5,1},{9,5},{13,9},{2,14},{6,2},{... | collective-permute-start | bytes 98312 | tf_op jit(solution)/shard_map/ppermute | solution.py:238
  147.8 3.1 %collective-permute-done.61 = f32[32,256]{1,0:T(8,128)S(1)} collective-permute-done((f32[32,256]{1,0:T(8,128)S(1)}, f32[32,256]{1,0:T(8,128)S(1)}, u32[]{:S(2)}, u32[]{:S(2)}) %collective-permute-start.61) | collective-permute-done | bytes 32800 | tf_op jit(solution)/shard_map/ppermute | solution.py:238
  (123 shorter events, 79.8 us)
Async XLA Ops:
  4.1 4.5 %collective-permute-start = (f32[2,1024]{1,0:T(2,128)S(1)}, f32[2,1024]{1,0:T(2,128)S(1)}, u32[]{:S(2)}, u32[]{:S(2)}) collective-permute-start(f32[2,1024]{1,0:T(2,128)S(1)} %shard_map.42.refs_3_), channel_id=1, source_target_pairs={{0,1},{1,2},{2,3},{3,0},{4,5},{5,6},{6,7},{7,4},{8,9},{9,10},{10,1... | collective-permute-start | bytes 24584 | tf_op jit(solution)/shard_map/ppermute | solution.py:231
  4.6 4.2 %collective-permute-start.1 = (f32[2,1024]{1,0:T(2,128)S(1)}, f32[2,1024]{1,0:T(2,128)S(1)}, u32[]{:S(2)}, u32[]{:S(2)}) collective-permute-start(f32[2,1024]{1,0:T(2,128)S(1)} %shard_map.42.refs_3_), channel_id=1, source_target_pairs={{0,2},{1,3},{2,0},{3,1},{4,6},{5,7},{6,4},{7,5},{8,10},{9,11},{10,... | collective-permute-start | bytes 24584 | tf_op jit(solution)/shard_map/ppermute | solution.py:231
  11.3 5.6 %collective-permute-start.3 = (f32[2,1024]{1,0:T(2,128)S(1)}, f32[2,1024]{1,0:T(2,128)S(1)}, u32[]{:S(2)}, u32[]{:S(2)}) collective-permute-start(f32[2,1024]{1,0:T(2,128)S(1)} %get-tuple-element.61.refs_3_), channel_id=1, source_target_pairs={{0,4},{4,8},{8,12},{12,0},{1,5},{5,9},{9,13},{13,1},{2,6},{6,10},{... | collective-permute-start | bytes 24584 | tf_op jit(solution)/shard_map/ppermute | solution.py:231
  12.9 4.5 %collective-permute-start.4 = (f32[2,1024]{1,0:T(2,128)S(1)}, f32[2,1024]{1,0:T(2,128)S(1)}, u32[]{:S(2)}, u32[]{:S(2)}) collective-permute-start(f32[2,1024]{1,0:T(2,128)S(1)} %get-tuple-element.61.refs_3_), channel_id=1, source_target_pairs={{0,8},{4,12},{8,0},{12,4},{1,9},{5,13},{9,1},{13,5},{2,10},{6,14},... | collective-permute-start | bytes 24584 | tf_op jit(solution)/shard_map/ppermute | solution.py:231
  20.6 3.8 %collective-permute-start.7 = (f32[2,1024]{1,0:T(2,128)S(1)}, f32[2,1024]{1,0:T(2,128)S(1)}, u32[]{:S(2)}, u32[]{:S(2)}) collective-permute-start(f32[2,1024]{1,0:T(2,128)S(1)} %get-tuple-element.62.refs_3_), channel_id=1, source_target_pairs={{0,2},{1,3},{2,0},{3,1},{4,6},{5,7},{6,4},{7,5},{8,10},{9,11},{10,... | collective-permute-start | bytes 24584 | tf_op jit(solution)/shard_map/ppermute | solution.py:231
  25.7 5.5 %collective-permute-start.9 = (f32[2,1024]{1,0:T(2,128)S(1)}, f32[2,1024]{1,0:T(2,128)S(1)}, u32[]{:S(2)}, u32[]{:S(2)}) collective-permute-start(f32[2,1024]{1,0:T(2,128)S(1)} %get-tuple-element.64.refs_3_), channel_id=1, source_target_pairs={{0,4},{4,8},{8,12},{12,0},{1,5},{5,9},{9,13},{13,1},{2,6},{6,10},{... | collective-permute-start | bytes 24584 | tf_op jit(solution)/shard_map/ppermute | solution.py:231
  26.0 5.2 %collective-permute-start.10 = (f32[2,1024]{1,0:T(2,128)S(1)}, f32[2,1024]{1,0:T(2,128)S(1)}, u32[]{:S(2)}, u32[]{:S(2)}) collective-permute-start(f32[2,1024]{1,0:T(2,128)S(1)} %get-tuple-element.64.refs_3_), channel_id=1, source_target_pairs={{0,8},{4,12},{8,0},{12,4},{1,9},{5,13},{9,1},{13,5},{2,10},{6,14},... | collective-permute-start | bytes 24584 | tf_op jit(solution)/shard_map/ppermute | solution.py:231
  34.6 3.7 %collective-permute-start.13 = (f32[2,1024]{1,0:T(2,128)S(1)}, f32[2,1024]{1,0:T(2,128)S(1)}, u32[]{:S(2)}, u32[]{:S(2)}) collective-permute-start(f32[2,1024]{1,0:T(2,128)S(1)} %get-tuple-element.65.refs_3_), channel_id=1, source_target_pairs={{0,2},{1,3},{2,0},{3,1},{4,6},{5,7},{6,4},{7,5},{8,10},{9,11},{10,... | collective-permute-start | bytes 24584 | tf_op jit(solution)/shard_map/ppermute | solution.py:231
  39.8 5.5 %collective-permute-start.15 = (f32[2,1024]{1,0:T(2,128)S(1)}, f32[2,1024]{1,0:T(2,128)S(1)}, u32[]{:S(2)}, u32[]{:S(2)}) collective-permute-start(f32[2,1024]{1,0:T(2,128)S(1)} %get-tuple-element.67.refs_3_), channel_id=1, source_target_pairs={{0,4},{4,8},{8,12},{12,0},{1,5},{5,9},{9,13},{13,1},{2,6},{6,10},{... | collective-permute-start | bytes 24584 | tf_op jit(solution)/shard_map/ppermute | solution.py:231
  40.5 4.8 %collective-permute-start.16 = (f32[2,1024]{1,0:T(2,128)S(1)}, f32[2,1024]{1,0:T(2,128)S(1)}, u32[]{:S(2)}, u32[]{:S(2)}) collective-permute-start(f32[2,1024]{1,0:T(2,128)S(1)} %get-tuple-element.67.refs_3_), channel_id=1, source_target_pairs={{0,8},{4,12},{8,0},{12,4},{1,9},{5,13},{9,1},{13,5},{2,10},{6,14},... | collective-permute-start | bytes 24584 | tf_op jit(solution)/shard_map/ppermute | solution.py:231
  47.4 3.7 %collective-permute-start.19 = (f32[2,1024]{1,0:T(2,128)S(1)}, f32[2,1024]{1,0:T(2,128)S(1)}, u32[]{:S(2)}, u32[]{:S(2)}) collective-permute-start(f32[2,1024]{1,0:T(2,128)S(1)} %get-tuple-element.68.refs_3_), channel_id=1, source_target_pairs={{0,2},{1,3},{2,0},{3,1},{4,6},{5,7},{6,4},{7,5},{8,10},{9,11},{10,... | collective-permute-start | bytes 24584 | tf_op jit(solution)/shard_map/ppermute | solution.py:231
  52.6 5.5 %collective-permute-start.21 = (f32[2,1024]{1,0:T(2,128)S(1)}, f32[2,1024]{1,0:T(2,128)S(1)}, u32[]{:S(2)}, u32[]{:S(2)}) collective-permute-start(f32[2,1024]{1,0:T(2,128)S(1)} %get-tuple-element.70.refs_3_), channel_id=1, source_target_pairs={{0,4},{4,8},{8,12},{12,0},{1,5},{5,9},{9,13},{13,1},{2,6},{6,10},{... | collective-permute-start | bytes 24584 | tf_op jit(solution)/shard_map/ppermute | solution.py:231
  54.5 4.5 %collective-permute-start.22 = (f32[2,1024]{1,0:T(2,128)S(1)}, f32[2,1024]{1,0:T(2,128)S(1)}, u32[]{:S(2)}, u32[]{:S(2)}) collective-permute-start(f32[2,1024]{1,0:T(2,128)S(1)} %get-tuple-element.70.refs_3_), channel_id=1, source_target_pairs={{0,8},{4,12},{8,0},{12,4},{1,9},{5,13},{9,1},{13,5},{2,10},{6,14},... | collective-permute-start | bytes 24584 | tf_op jit(solution)/shard_map/ppermute | solution.py:231
  61.4 3.7 %collective-permute-start.25 = (f32[2,1024]{1,0:T(2,128)S(1)}, f32[2,1024]{1,0:T(2,128)S(1)}, u32[]{:S(2)}, u32[]{:S(2)}) collective-permute-start(f32[2,1024]{1,0:T(2,128)S(1)} %get-tuple-element.71.refs_3_), channel_id=1, source_target_pairs={{0,2},{1,3},{2,0},{3,1},{4,6},{5,7},{6,4},{7,5},{8,10},{9,11},{10,... | collective-permute-start | bytes 24584 | tf_op jit(solution)/shard_map/ppermute | solution.py:231
  66.6 5.5 %collective-permute-start.27 = (f32[2,1024]{1,0:T(2,128)S(1)}, f32[2,1024]{1,0:T(2,128)S(1)}, u32[]{:S(2)}, u32[]{:S(2)}) collective-permute-start(f32[2,1024]{1,0:T(2,128)S(1)} %get-tuple-element.77.refs_0_), channel_id=1, source_target_pairs={{0,4},{4,8},{8,12},{12,0},{1,5},{5,9},{9,13},{13,1},{2,6},{6,10},{... | collective-permute-start | bytes 24584 | tf_op jit(solution)/shard_map/ppermute | solution.py:231
  67.4 4.8 %collective-permute-start.28 = (f32[2,1024]{1,0:T(2,128)S(1)}, f32[2,1024]{1,0:T(2,128)S(1)}, u32[]{:S(2)}, u32[]{:S(2)}) collective-permute-start(f32[2,1024]{1,0:T(2,128)S(1)} %get-tuple-element.77.refs_0_), channel_id=1, source_target_pairs={{0,8},{4,12},{8,0},{12,4},{1,9},{5,13},{9,1},{13,5},{2,10},{6,14},... | collective-permute-start | bytes 24584 | tf_op jit(solution)/shard_map/ppermute | solution.py:231
  74.3 3.7 %collective-permute-start.31 = (f32[1,1024]{1,0:T(1,128)S(1)}, f32[1,1024]{1,0:T(1,128)S(1)}, u32[]{:S(2)}, u32[]{:S(2)}) collective-permute-start(f32[1,1024]{1,0:T(1,128)S(1)} %get-tuple-element.79.refs_0_), channel_id=1, source_target_pairs={{0,2},{1,3},{2,0},{3,1},{4,6},{5,7},{6,4},{7,5},{8,10},{9,11},{10,... | collective-permute-start | bytes 12296 | tf_op jit(solution)/shard_map/ppermute | solution.py:231
  79.0 5.5 %collective-permute-start.33 = (f32[1,1024]{1,0:T(1,128)S(1)}, f32[1,1024]{1,0:T(1,128)S(1)}, u32[]{:S(2)}, u32[]{:S(2)}) collective-permute-start(f32[1,1024]{1,0:T(1,128)S(1)} %get-tuple-element.80.refs_0_), channel_id=1, source_target_pairs={{0,4},{4,8},{8,12},{12,0},{1,5},{5,9},{9,13},{13,1},{2,6},{6,10},{... | collective-permute-start | bytes 12296 | tf_op jit(solution)/shard_map/ppermute | solution.py:231
  80.5 4.5 %collective-permute-start.34 = (f32[1,1024]{1,0:T(1,128)S(1)}, f32[1,1024]{1,0:T(1,128)S(1)}, u32[]{:S(2)}, u32[]{:S(2)}) collective-permute-start(f32[1,1024]{1,0:T(1,128)S(1)} %get-tuple-element.80.refs_0_), channel_id=1, source_target_pairs={{0,8},{4,12},{8,0},{12,4},{1,9},{5,13},{9,1},{13,5},{2,10},{6,14},... | collective-permute-start | bytes 12296 | tf_op jit(solution)/shard_map/ppermute | solution.py:231
  91.8 5.5 %collective-permute-start.39 = (f32[1,1024]{1,0:T(1,128)S(1)}, f32[1,1024]{1,0:T(1,128)S(1)}, u32[]{:S(2)}, u32[]{:S(2)}) collective-permute-start(f32[1,1024]{1,0:T(1,128)S(1)} %get-tuple-element.82.refs_0_), channel_id=1, source_target_pairs={{0,4},{4,8},{8,12},{12,0},{1,5},{5,9},{9,13},{13,1},{2,6},{6,10},{... | collective-permute-start | bytes 12296 | tf_op jit(solution)/shard_map/ppermute | solution.py:231
  92.8 4.6 %collective-permute-start.40 = (f32[1,1024]{1,0:T(1,128)S(1)}, f32[1,1024]{1,0:T(1,128)S(1)}, u32[]{:S(2)}, u32[]{:S(2)}) collective-permute-start(f32[1,1024]{1,0:T(1,128)S(1)} %get-tuple-element.82.refs_0_), channel_id=1, source_target_pairs={{0,8},{4,12},{8,0},{12,4},{1,9},{5,13},{9,1},{13,5},{2,10},{6,14},... | collective-permute-start | bytes 12296 | tf_op jit(solution)/shard_map/ppermute | solution.py:231
  99.2 3.7 %collective-permute-start.43 = (f32[1,1024]{1,0:T(1,128)S(1)}, f32[1,1024]{1,0:T(1,128)S(1)}, u32[]{:S(2)}, u32[]{:S(2)}) collective-permute-start(f32[1,1024]{1,0:T(1,128)S(1)} %get-tuple-element.83.refs_0_), channel_id=1, source_target_pairs={{0,2},{1,3},{2,0},{3,1},{4,6},{5,7},{6,4},{7,5},{8,10},{9,11},{10,... | collective-permute-start | bytes 12296 | tf_op jit(solution)/shard_map/ppermute | solution.py:231
  103.9 5.5 %collective-permute-start.45 = (f32[1,1024]{1,0:T(1,128)S(1)}, f32[1,1024]{1,0:T(1,128)S(1)}, u32[]{:S(2)}, u32[]{:S(2)}) collective-permute-start(f32[1,1024]{1,0:T(1,128)S(1)} %get-tuple-element.84.refs_0_), channel_id=1, source_target_pairs={{0,4},{4,8},{8,12},{12,0},{1,5},{5,9},{9,13},{13,1},{2,6},{6,10},{... | collective-permute-start | bytes 12296 | tf_op jit(solution)/shard_map/ppermute | solution.py:231
  105.5 4.5 %collective-permute-start.46 = (f32[1,1024]{1,0:T(1,128)S(1)}, f32[1,1024]{1,0:T(1,128)S(1)}, u32[]{:S(2)}, u32[]{:S(2)}) collective-permute-start(f32[1,1024]{1,0:T(1,128)S(1)} %get-tuple-element.84.refs_0_), channel_id=1, source_target_pairs={{0,8},{4,12},{8,0},{12,4},{1,9},{5,13},{9,1},{13,5},{2,10},{6,14},... | collective-permute-start | bytes 12296 | tf_op jit(solution)/shard_map/ppermute | solution.py:231
  112.0 3.7 %collective-permute-start.49 = (f32[1,1024]{1,0:T(1,128)S(1)}, f32[1,1024]{1,0:T(1,128)S(1)}, u32[]{:S(2)}, u32[]{:S(2)}) collective-permute-start(f32[1,1024]{1,0:T(1,128)S(1)} %get-tuple-element.85.refs_0_), channel_id=1, source_target_pairs={{0,2},{1,3},{2,0},{3,1},{4,6},{5,7},{6,4},{7,5},{8,10},{9,11},{10,... | collective-permute-start | bytes 12296 | tf_op jit(solution)/shard_map/ppermute | solution.py:231
  116.7 5.5 %collective-permute-start.51 = (f32[1,1024]{1,0:T(1,128)S(1)}, f32[1,1024]{1,0:T(1,128)S(1)}, u32[]{:S(2)}, u32[]{:S(2)}) collective-permute-start(f32[1,1024]{1,0:T(1,128)S(1)} %get-tuple-element.86.refs_0_), channel_id=1, source_target_pairs={{0,4},{4,8},{8,12},{12,0},{1,5},{5,9},{9,13},{13,1},{2,6},{6,10},{... | collective-permute-start | bytes 12296 | tf_op jit(solution)/shard_map/ppermute | solution.py:231
  117.7 4.5 %collective-permute-start.52 = (f32[1,1024]{1,0:T(1,128)S(1)}, f32[1,1024]{1,0:T(1,128)S(1)}, u32[]{:S(2)}, u32[]{:S(2)}) collective-permute-start(f32[1,1024]{1,0:T(1,128)S(1)} %get-tuple-element.86.refs_0_), channel_id=1, source_target_pairs={{0,8},{4,12},{8,0},{12,4},{1,9},{5,13},{9,1},{13,5},{2,10},{6,14},... | collective-permute-start | bytes 12296 | tf_op jit(solution)/shard_map/ppermute | solution.py:231
  141.8 4.2 %collective-permute-start.59 = (f32[32,256]{1,0:T(8,128)S(1)}, f32[32,256]{1,0:T(8,128)S(1)}, u32[]{:S(2)}, u32[]{:S(2)}) collective-permute-start(f32[32,256]{1,0:T(8,128)S(1)} %get-tuple-element.99), channel_id=1, source_target_pairs={{0,3},{1,0},{2,1},{3,2},{4,7},{5,4},{6,5},{7,6},{8,11},{9,8},{10,9... | collective-permute-start | bytes 98312 | tf_op jit(solution)/shard_map/ppermute | solution.py:238
  141.9 4.7 %collective-permute-start.58 = (f32[32,256]{1,0:T(8,128)S(1)}, f32[32,256]{1,0:T(8,128)S(1)}, u32[]{:S(2)}, u32[]{:S(2)}) collective-permute-start(f32[32,256]{1,0:T(8,128)S(1)} %get-tuple-element.98), channel_id=1, source_target_pairs={{0,2},{1,3},{2,0},{3,1},{4,6},{5,7},{6,4},{7,5},{8,10},{9,11},{10,... | collective-permute-start | bytes 98312 | tf_op jit(solution)/shard_map/ppermute | solution.py:238
  143.1 4.6 %collective-permute-start.62 = (f32[32,256]{1,0:T(8,128)S(1)}, f32[32,256]{1,0:T(8,128)S(1)}, u32[]{:S(2)}, u32[]{:S(2)}) collective-permute-start(f32[32,256]{1,0:T(8,128)S(1)} %get-tuple-element.103), channel_id=1, source_target_pairs={{0,12},{4,0},{8,4},{12,8},{1,13},{5,1},{9,5},{13,9},{2,14},{6,2},{... | collective-permute-start | bytes 98312 | tf_op jit(solution)/shard_map/ppermute | solution.py:238
  146.0 4.8 %collective-permute-start.61 = (f32[32,256]{1,0:T(8,128)S(1)}, f32[32,256]{1,0:T(8,128)S(1)}, u32[]{:S(2)}, u32[]{:S(2)}) collective-permute-start(f32[32,256]{1,0:T(8,128)S(1)} %get-tuple-element.102), channel_id=1, source_target_pairs={{0,8},{4,12},{8,0},{12,4},{1,9},{5,13},{9,1},{13,5},{2,10},{6,14},... | collective-permute-start | bytes 98312 | tf_op jit(solution)/shard_map/ppermute | solution.py:238
  146.0 5.7 %collective-permute-start.60 = (f32[32,256]{1,0:T(8,128)S(1)}, f32[32,256]{1,0:T(8,128)S(1)}, u32[]{:S(2)}, u32[]{:S(2)}) collective-permute-start(f32[32,256]{1,0:T(8,128)S(1)} %get-tuple-element.101), channel_id=1, source_target_pairs={{0,4},{4,8},{8,12},{12,0},{1,5},{5,9},{9,13},{13,1},{2,6},{6,10},{... | collective-permute-start | bytes 98312 | tf_op jit(solution)/shard_map/ppermute | solution.py:238
  (33 other events, 99.4 us)

commit v2 on v1

v2 whole, which is shorter than its diff:
```python
import functools
import math

import jax
import jax.numpy as jnp
from jax import lax
from jax.experimental import pallas as pl
from jax.experimental.pallas import tpu as pltpu
from jax.sharding import PartitionSpec as P

ITERS = 5
EPSILON = 0.05
SCALE = 1.0 / (EPSILON * math.log(2.0))
DEPTH = 256
CHUNK = 256
F32 = jnp.float32
BF16 = jnp.bfloat16
VMEM_LIMIT = 48 * 1024 * 1024


def split3(v):
    high = v.astype(BF16).astype(F32)
    rest = v - high
    mid = rest.astype(BF16).astype(F32)
    low = (rest - mid).astype(BF16).astype(F32)
    return high, mid, low


def vmem(count):
    return [pl.BlockSpec(memory_space=pltpu.VMEM)] * count


def call(body, outs, count, scratch=()):
    return pl.pallas_call(
        body,
        out_shape=outs,
        in_specs=vmem(count),
        out_specs=vmem(len(outs)),
        scratch_shapes=list(scratch),
        compiler_params=pltpu.CompilerParams(vmem_limit_bytes=VMEM_LIMIT),
    )


def shape(dims, dtype=F32):
    return jax.ShapeDtypeStruct(dims, dtype)


def factors(points, order):
    parts = split3(points)
    width = points.shape[1]
    blocks = [parts[o] for o in order]
    zero16 = jnp.zeros((16, width), F32)
    tail = jnp.zeros((DEPTH - 144 - 2 * points.shape[0], width), F32)
    return jnp.concatenate(blocks[:4] + [zero16] + blocks[4:] + [tail], axis=0)


X_ORDER = (0, 0, 1, 0, 2, 1)
Y_ORDER = (0, 1, 0, 2, 0, 1)


def prepare_body(x_hbm, y_hbm, ax0, ax1, ay0, ay1, bx, by, start_ref, out, x_ref, y_ref, sems):
    copies = [
        pltpu.make_async_copy(x_hbm, x_ref, sems.at[0]),
        pltpu.make_async_copy(y_hbm, y_ref, sems.at[1]),
    ]
    for copy in copies:
        copy.start()
    for copy in copies:
        copy.wait()
    x = x_ref[...]
    y = y_ref[...]
    xf = factors(x * (2.0 * SCALE), X_ORDER)
    yf = factors(y, Y_ORDER)
    for factor, left0, left1, right in ((xf, ax0, ax1, bx), (yf, ay0, ay1, by)):
        right[...] = factor.astype(BF16)
        turned = factor.T
        left0[...] = turned[:, :128].astype(BF16)
        left1[...] = turned[:, 128:]
    start = -SCALE * jnp.sum(y * y, axis=0, keepdims=True)
    start_ref[...] = start
    left, unused = left_factor(ay0, ay1, start)
    partial_lse(left, bx, out)


def left_factor(left0, left1, pot, adj=None):
    width = pot.shape[1]
    high, mid, low = split3(pot)
    one = jnp.ones((1, width), F32)
    rows = [high, mid, low, one, one, one, jnp.zeros_like(one)]
    rows.append(jnp.zeros_like(one) if adj is None else adj)
    rows.append(jnp.zeros((120, width), F32))
    turned = jnp.concatenate(rows, axis=0).T
    column = None
    if adj is not None:
        column = turned[:, 7:8]
        lane = lax.broadcasted_iota(jnp.int32, turned.shape, 1)
        turned = jnp.where(lane == 7, 0.0, turned)
    return jnp.concatenate([left0[...], (left1[...] + turned).astype(BF16)], axis=1), column


def right_rows(pot):
    width = pot.shape[1]
    one = jnp.ones((3, width), F32)
    high, mid, low = split3(pot)
    return jnp.concatenate([one, high, mid, low, jnp.zeros((10, width), F32)], axis=0).astype(BF16)


def right_chunk(right, rows, at, wide):
    return jnp.concatenate(
        [right[0:128, at : at + wide], rows[:, at : at + wide], right[144:DEPTH, at : at + wide]], axis=0
    )


def matmul(a, b):
    return jnp.dot(a, b, preferred_element_type=F32)


def send(out, at, wide, value):
    for d in range(out.shape[0]):
        out[d, :, at : at + wide] = value


def partial_lse(left, right, out):
    width = right.shape[1]
    rows = right_rows(jnp.zeros((1, width), F32))
    wide = min(CHUNK, width)
    for at in range(0, width, wide):
        scores = matmul(left, right_chunk(right, rows, at, wide))
        top = jnp.max(scores, axis=0, keepdims=True)
        total = jnp.sum(jnp.exp2(scores - top), axis=0, keepdims=True)
        send(out, at, wide, top + jnp.log2(total))


def join_lse(got, log_mass):
    parts = [got[d] for d in range(got.shape[0])]
    top = functools.reduce(jnp.maximum, parts)
    total = sum(jnp.exp2(p - top) for p in parts)
    return log_mass - (top + jnp.log2(total))


def join_sum(got):
    return sum(got[d] for d in range(got.shape[0]))


def forward_body(log_mass, left0, left1, right, got, pot_out, out):
    pot = join_lse(got, log_mass)
    pot_out[...] = pot
    left, unused = left_factor(left0, left1, pot)
    partial_lse(left, right, out)


def weighted_sums(left, column, right, rows, out):
    width = right.shape[1]
    wide = min(CHUNK, width)
    for at in range(0, width, wide):
        scores = matmul(left, right_chunk(right, rows, at, wide))
        send(out, at, wide, jnp.sum(jnp.exp2(scores) * column, axis=0, keepdims=True))


def turn_body(log_mass, log_scale, left0, left1, right, pot_right, got, pot_out, out):
    pot = join_lse(got, log_mass)
    pot_out[...] = pot
    left, column = left_factor(left0, left1, pot, jnp.ones_like(pot))
    weighted_sums(left, column, right, right_rows(pot_right[...] + log_scale), out)


def backward_body(leading, log_scale, left0, left1, right, pot_left, pot_right, got, adj_out, out):
    adj = leading - join_sum(got)
    adj_out[...] = adj
    left, column = left_factor(left0, left1, pot_left[...], adj)
    weighted_sums(left, column, right, right_rows(pot_right[...] + log_scale), out)


SPREAD = 30.0
STRIP = 256


def gradient_body(dim, log_cols, log_rows, ax0, ax1, by, x_ref, y_ref, *refs):
    pots_rows = refs[:ITERS]
    pots_cols = refs[ITERS : 2 * ITERS + 1]
    adjs_rows = refs[2 * ITERS + 1 : 3 * ITERS]
    adjs_cols = refs[3 * ITERS : 4 * ITERS - 1]
    got, out_x, out_y, cols_rows, x_parts, y_parts, gx, gy, left_e, left_r, right_r = refs[4 * ITERS - 1 :]
    count_rows, count_cols = x_ref.shape[1], y_ref.shape[1]
    us = [p[...] for p in pots_rows]
    vs = [p[...] for p in pots_cols]
    first = (1.0 if ITERS == 1 else 0.0) - join_sum(got)
    adjs_rows = [first] + [a[...] for a in adjs_rows]
    adjs_cols = [a[...] for a in adjs_cols] + [jnp.ones((1, count_cols), F32)]
    shift = log_rows - log_cols

    x = x_ref[...]
    y = y_ref[...]
    one = jnp.ones((1, count_cols), F32)
    pad = jnp.zeros((31, count_cols), F32)
    y_parts[...] = jnp.concatenate(list(split3(y)) + [one, pad], axis=0).T.astype(BF16)
    one = jnp.ones((1, count_rows), F32)
    pad = jnp.zeros((31, count_rows), F32)
    x_parts[...] = jnp.concatenate(list(split3(x)) + [one, pad], axis=0).astype(BF16)
    gy[...] = jnp.zeros_like(gy)

    far_u = functools.reduce(jnp.maximum, [jnp.abs(u - us[-1]) for u in us])
    far_v = functools.reduce(jnp.maximum, [jnp.abs(v - vs[-1]) for v in vs])
    near = jnp.maximum(jnp.max(far_u), jnp.max(far_v)) < SPREAD

    def add_strip(at, total):
        upper = total.astype(BF16)
        lower = (total - upper.astype(F32)).astype(BF16)
        gx[at, :] = matmul(upper, y_parts[...]) + matmul(lower, y_parts[...])
        gy[...] += matmul(x_parts[:, at], upper) + matmul(x_parts[:, at], lower)

    @pl.when(near)
    def factored():
        alpha = [jnp.exp2(u - us[-1]) for u in us]
        beta = [jnp.exp2(v - vs[-1]) for v in vs]
        p_rows = alpha + [a * adj for a, adj in zip(alpha, adjs_rows)]
        q_rows = [b * adj for b, adj in zip(beta[1:], adjs_cols)] + [b * 2.0**shift for b in beta[:-1]]
        fill = 16 - 2 * ITERS
        p_split = split3(jnp.concatenate(p_rows + [jnp.zeros((fill, count_rows), F32)], axis=0))
        q_split = split3(jnp.concatenate(q_rows + [jnp.zeros((fill, count_cols), F32)], axis=0))
        tail = [jnp.zeros((32, count_rows), F32)]
        left_r[...] = jnp.concatenate([p_split[o] for o in X_ORDER] + tail, axis=0).T.astype(BF16)
        tail = [jnp.zeros((32, count_cols), F32)]
        right_r[...] = jnp.concatenate([q_split[o] for o in Y_ORDER] + tail, axis=0).astype(BF16)
        left, unused = left_factor(ax0, ax1, us[-1] + log_cols)
        left_e[...] = left
        right = right_chunk(by, right_rows(vs[-1]), 0, count_cols)
        strip = min(STRIP, count_rows)
        for step in range(count_rows // strip):
            at = pl.ds(step * strip, strip)
            total = jnp.exp2(matmul(left_e[at, :], right)) * matmul(left_r[at, :], right_r[...])
            add_strip(at, total)

    @pl.when(jnp.logical_not(near))
    def separate():
        stack = [u + log_cols for u in us] + adjs_rows
        stack.append(jnp.zeros((128 - len(stack), count_rows), F32))
        cols_rows[...] = jnp.concatenate(stack, axis=0).T
        strip = 128

        def block(step, carry):
            at = pl.ds(pl.multiple_of(step * strip, strip), strip)
            left = jnp.concatenate([ax0[at, :], ax1[at, :].astype(BF16)], axis=1)
            inner = matmul(left, by[...])
            columns = cols_rows[at, :]
            total = jnp.zeros_like(inner)
            for k in range(ITERS):
                base = inner + columns[:, k : k + 1]
                total += jnp.exp2(base + vs[k + 1]) * adjs_cols[k]
                total += jnp.exp2(base + (vs[k] + shift)) * columns[:, ITERS + k : ITERS + k + 1]
            add_strip(at, total)
            return carry

        lax.fori_loop(0, count_rows // strip, block, 0)

    def finish(points, sums):
        mixed = sums[0:dim] + sums[dim : 2 * dim] + sums[2 * dim : 3 * dim]
        return 2.0 * (points * sums[3 * dim : 3 * dim + 1] - mixed)

    for value, out in ((finish(x, gx[...].T), out_x), (finish(y, gy[...]), out_y)):
        share = out.shape[2]
        for p in range(out.shape[0]):
            out[p] = value[:, p * share : (p + 1) * share]


def exchange(value, axis):
    return lax.all_to_all(value, axis, 0, 0, tiled=True)


def on_device(x_points, y_points):
    x = x_points.T
    y = y_points.T
    dim, count_rows = x.shape
    count_cols = y.shape[1]
    n_row, n_col = lax.axis_size("row"), lax.axis_size("col")
    log_rows = math.log2(count_rows * n_row)
    log_cols = math.log2(count_cols * n_col)
    row, col = (1, count_rows), (1, count_cols)
    to_col, to_row = shape((n_col,) + row), shape((n_row,) + col)

    ax0, ax1, ay0, ay1, bx, by, start, part = pl.pallas_call(
        prepare_body,
        out_shape=[
            shape((count_rows, 128), BF16),
            shape((count_rows, 128)),
            shape((count_cols, 128), BF16),
            shape((count_cols, 128)),
            shape((DEPTH, count_rows), BF16),
            shape((DEPTH, count_cols), BF16),
            shape(col),
            to_col,
        ],
        in_specs=[pl.BlockSpec(memory_space=pl.ANY)] * 2,
        out_specs=vmem(8),
        scratch_shapes=[pltpu.VMEM(x.shape, F32), pltpu.VMEM(y.shape, F32), pltpu.SemaphoreType.DMA((2,))],
        compiler_params=pltpu.CompilerParams(vmem_limit_bytes=VMEM_LIMIT),
    )(x, y)

    pots_rows, pots_cols = [], [start]
    for k in range(ITERS):
        got = exchange(part, "col")
        pot, part = call(functools.partial(forward_body, -log_rows), [shape(row), to_row], 4)(ax0, ax1, by, got)
        pots_rows.append(pot)
        got = exchange(part, "row")
        if k < ITERS - 1:
            pot, part = call(functools.partial(forward_body, -log_cols), [shape(col), to_col], 4)(
                ay0, ay1, bx, got
            )
            pots_cols.append(pot)
    pot, part = call(functools.partial(turn_body, -log_cols, log_cols), [shape(col), to_col], 5)(
        ay0, ay1, bx, pots_rows[-1], got
    )
    pots_cols.append(pot)

    adjs_rows, adjs_cols = [], []
    for k in reversed(range(1, ITERS)):
        leading = 1.0 if k == ITERS - 1 else 0.0
        got = exchange(part, "col")
        adj, part = call(functools.partial(backward_body, leading, log_rows), [shape(row), to_row], 6)(
            ax0, ax1, by, pots_rows[k], pots_cols[k], got
        )
        adjs_rows.insert(0, adj)
        got = exchange(part, "row")
        adj, part = call(functools.partial(backward_body, 0.0, log_cols), [shape(col), to_col], 6)(
            ay0, ay1, bx, pots_cols[k], pots_rows[k - 1], got
        )
        adjs_cols.insert(0, adj)
    got = exchange(part, "col")

    out_x, out_y = call(
        functools.partial(gradient_body, dim, log_cols, log_rows),
        [shape((n_col, dim, count_rows // n_col)), shape((n_row, dim, count_cols // n_row))],
        5 + 4 * ITERS,
        [
            pltpu.VMEM((count_rows, 128), F32),
            pltpu.VMEM((128, count_rows), BF16),
            pltpu.VMEM((count_cols, 128), BF16),
            pltpu.VMEM((count_rows, 128), F32),
            pltpu.VMEM((128, count_cols), F32),
            pltpu.VMEM((count_rows, DEPTH), BF16),
            pltpu.VMEM((count_rows, 128), BF16),
            pltpu.VMEM((128, count_cols), BF16),
        ],
    )(ax0, ax1, by, x, y, *pots_rows, *pots_cols, *adjs_rows, *adjs_cols, got)
    grad_x = jnp.sum(exchange(out_x, "col"), axis=0)
    grad_y = jnp.sum(exchange(out_y, "row"), axis=0)
    return (grad_x.T, grad_y.T)


def solution(mesh):
    in_specs = (P(("groups", "row"), None), P(("groups", "col"), None))
    out_specs = (P(("groups", "row", "col"), None), P(("groups", "col", "row"), None))
    return jax.shard_map(
        on_device, mesh=mesh, in_specs=in_specs, out_specs=out_specs, check_vma=False
    )
```

time: 153 us -> 184 us (1.20)
  blocking collectives: 0 us -> 145 us
  starting transfers between devices: 68.4 us -> 3.32 us
  waiting for transfers between devices: 44.6 us -> 5.41 us
  Pallas kernels: 35.4 us -> 26.1 us
    all_to_all x0 -> x20, blocking collectives: none -> 145 us  [exchange(): return lax.all_to_all(value, axis, 0, 0, tiled=True)]
    ppermute x63 -> x0, starting transfers between devices: 68.4 us -> none  [the longest x57 63.6 us: exchange(): lax.ppermute(value, axis, [(d, (d + s) % size) for d in range(size)])]
    ppermute x63 -> x0, waiting for transfers between devices: 44.6 us -> none  [the longest x57 40.1 us: exchange(): lax.ppermute(value, axis, [(d, (d + s) % size) for d in range(size)])]
    pallas_call x21 -> x20, Pallas kernels: 35.4 us -> 26.1 us  [the longest x5 6.66 us: on_device(): call(functools.partial(forward_body, -log_rows), [shape(row), to_row], 4)]
    all_to_all x0 -> x1, waiting for transfers between devices: none -> 5.41 us  [exchange(): return lax.all_to_all(value, axis, 0, 0, tiled=True)]
    all_to_all x0 -> x1, starting transfers between devices: none -> 3.32 us  [exchange(): return lax.all_to_all(value, axis, 0, 0, tiled=True)]
  transfers between devices with their start and end apart: 63 -> 1, of which waited for: 54 -> 1; matrix products, arithmetic and copies ran while one was open for 0% -> 0% of each run, Pallas kernels for 0% -> 0%
where the time goes in v2:
time: 184 us; the launch traced here: 183 us
  blocking collectives  145 us (79%)
  Pallas kernels  26.1 us (14%)
  waiting for transfers between devices  5.41 us (3%)
  starting transfers between devices  3.32 us (2%)
    all_to_all x20, blocking collectives, exchange(): return lax.all_to_all(value, axis, 0, 0, tiled=True)  145 us
    pallas_call x5, Pallas kernels, on_device(): call(functools.partial(forward_body, -log_rows), [shape(row), to_row], 4)  6.66 us
    all_to_all x1, waiting for transfers between devices, exchange(): return lax.all_to_all(value, axis, 0, 0, tiled=True)  5.41 us
    pallas_call x4, Pallas kernels, on_device(): call(functools.partial(forward_body, -log_cols), [shape(col), to_col], 4)  5.31 us
    pallas_call x1, Pallas kernels, on_device(): call(functools.partial(gradient_body, dim, log_cols, log_rows), [shape((n...  4.31 us
  transfers between devices with their start and end apart: 1, of which 1 were waited for; matrix products, arithmetic and copies ran while one was open for 0% of the time, Pallas kernels for 0%

profile of v2, /device:TPU:0, one launch (start us, length us, event | category | flops | bytes accessed | tf_op | source)
XLA Modules:
  0.0 183.3 jit_solution(8667459757552330899)
XLA Ops:
  2.4 1.7 shard_map.41
  4.2 7.9 %all_to_all.105.got = f32[4,1,1024]{2,1,0:T(1,128)S(1)} all-to-all(f32[4,1,1024]{2,1,0:T(1,128)S(1)} %get-tuple-element.51), channel_id=1, replica_groups=mesh['groups'=2,'row'=4,'col'=4] {'col'}, dimensions={0} | all-to-all | bytes 32768 | tf_op jit(solution)/shard_map/all_to_all | solution.py:267
  12.0 1.3 shard_map.42
  13.4 10.3 %all_to_all.106.got = f32[4,1,1024]{2,1,0:T(1,128)S(1)} all-to-all(f32[4,1,1024]{2,1,0:T(1,128)S(1)} %get-tuple-element.56), channel_id=1, replica_groups=mesh['groups'=2,'row'=4,'col'=4] {'row'}, dimensions={0} | all-to-all | bytes 32768 | tf_op jit(solution)/shard_map/all_to_all | solution.py:267
  23.6 1.3 shard_map.43
  25.0 6.2 %all_to_all.107.got = f32[4,1,1024]{2,1,0:T(1,128)S(1)} all-to-all(f32[4,1,1024]{2,1,0:T(1,128)S(1)} %get-tuple-element.57), channel_id=1, replica_groups=mesh['groups'=2,'row'=4,'col'=4] {'col'}, dimensions={0} | all-to-all | bytes 32768 | tf_op jit(solution)/shard_map/all_to_all | solution.py:267
  31.2 1.3 shard_map.44
  32.5 8.0 %all_to_all.108.got = f32[4,1,1024]{2,1,0:T(1,128)S(1)} all-to-all(f32[4,1,1024]{2,1,0:T(1,128)S(1)} %get-tuple-element.59), channel_id=1, replica_groups=mesh['groups'=2,'row'=4,'col'=4] {'row'}, dimensions={0} | all-to-all | bytes 32768 | tf_op jit(solution)/shard_map/all_to_all | solution.py:267
  40.5 1.3 shard_map.45
  41.8 6.2 %all_to_all.109.got = f32[4,1,1024]{2,1,0:T(1,128)S(1)} all-to-all(f32[4,1,1024]{2,1,0:T(1,128)S(1)} %get-tuple-element.60), channel_id=1, replica_groups=mesh['groups'=2,'row'=4,'col'=4] {'col'}, dimensions={0} | all-to-all | bytes 32768 | tf_op jit(solution)/shard_map/all_to_all | solution.py:267
  48.0 1.3 shard_map.46
  49.3 8.0 %all_to_all.110.got = f32[4,1,1024]{2,1,0:T(1,128)S(1)} all-to-all(f32[4,1,1024]{2,1,0:T(1,128)S(1)} %get-tuple-element.62), channel_id=1, replica_groups=mesh['groups'=2,'row'=4,'col'=4] {'row'}, dimensions={0} | all-to-all | bytes 32768 | tf_op jit(solution)/shard_map/all_to_all | solution.py:267
  58.6 6.2 %all_to_all.111.got = f32[4,1,1024]{2,1,0:T(1,128)S(1)} all-to-all(f32[4,1,1024]{2,1,0:T(1,128)S(1)} %get-tuple-element.63), channel_id=1, replica_groups=mesh['groups'=2,'row'=4,'col'=4] {'col'}, dimensions={0} | all-to-all | bytes 32768 | tf_op jit(solution)/shard_map/all_to_all | solution.py:267
  64.8 1.3 shard_map.48
  66.2 8.0 %all_to_all.112.got = f32[4,1,1024]{2,1,0:T(1,128)S(1)} all-to-all(f32[4,1,1024]{2,1,0:T(1,128)S(1)} %get-tuple-element.65), channel_id=1, replica_groups=mesh['groups'=2,'row'=4,'col'=4] {'row'}, dimensions={0} | all-to-all | bytes 32768 | tf_op jit(solution)/shard_map/all_to_all | solution.py:267
  74.1 1.3 shard_map.49
  75.5 6.2 %all_to_all.113.got = f32[4,1,1024]{2,1,0:T(1,128)S(1)} all-to-all(f32[4,1,1024]{2,1,0:T(1,128)S(1)} %get-tuple-element.66), channel_id=1, replica_groups=mesh['groups'=2,'row'=4,'col'=4] {'col'}, dimensions={0} | all-to-all | bytes 32768 | tf_op jit(solution)/shard_map/all_to_all | solution.py:267
  81.7 1.3 shard_map.50
  83.0 8.0 %all_to_all.114.got = f32[4,1,1024]{2,1,0:T(1,128)S(1)} all-to-all(f32[4,1,1024]{2,1,0:T(1,128)S(1)} %get-tuple-element.73), channel_id=1, replica_groups=mesh['groups'=2,'row'=4,'col'=4] {'row'}, dimensions={0} | all-to-all | bytes 32768 | tf_op jit(solution)/shard_map/all_to_all | solution.py:267
  91.9 6.2 %all_to_all.115.got = f32[4,1,1024]{2,1,0:T(1,128)S(1)} all-to-all(f32[4,1,1024]{2,1,0:T(1,128)S(1)} %get-tuple-element.75), channel_id=1, replica_groups=mesh['groups'=2,'row'=4,'col'=4] {'col'}, dimensions={0} | all-to-all | bytes 32768 | tf_op jit(solution)/shard_map/all_to_all | solution.py:267
  99.0 8.0 %all_to_all.116.got = f32[4,1,1024]{2,1,0:T(1,128)S(1)} all-to-all(f32[4,1,1024]{2,1,0:T(1,128)S(1)} %get-tuple-element.76), channel_id=1, replica_groups=mesh['groups'=2,'row'=4,'col'=4] {'row'}, dimensions={0} | all-to-all | bytes 32768 | tf_op jit(solution)/shard_map/all_to_all | solution.py:267
  107.9 6.2 %all_to_all.117.got = f32[4,1,1024]{2,1,0:T(1,128)S(1)} all-to-all(f32[4,1,1024]{2,1,0:T(1,128)S(1)} %get-tuple-element.77), channel_id=1, replica_groups=mesh['groups'=2,'row'=4,'col'=4] {'col'}, dimensions={0} | all-to-all | bytes 32768 | tf_op jit(solution)/shard_map/all_to_all | solution.py:267
  115.0 8.0 %all_to_all.118.got = f32[4,1,1024]{2,1,0:T(1,128)S(1)} all-to-all(f32[4,1,1024]{2,1,0:T(1,128)S(1)} %get-tuple-element.78), channel_id=1, replica_groups=mesh['groups'=2,'row'=4,'col'=4] {'row'}, dimensions={0} | all-to-all | bytes 32768 | tf_op jit(solution)/shard_map/all_to_all | solution.py:267
  123.9 6.2 %all_to_all.119.got = f32[4,1,1024]{2,1,0:T(1,128)S(1)} all-to-all(f32[4,1,1024]{2,1,0:T(1,128)S(1)} %get-tuple-element.79), channel_id=1, replica_groups=mesh['groups'=2,'row'=4,'col'=4] {'col'}, dimensions={0} | all-to-all | bytes 32768 | tf_op jit(solution)/shard_map/all_to_all | solution.py:267
  131.0 8.0 %all_to_all.120.got = f32[4,1,1024]{2,1,0:T(1,128)S(1)} all-to-all(f32[4,1,1024]{2,1,0:T(1,128)S(1)} %get-tuple-element.80), channel_id=1, replica_groups=mesh['groups'=2,'row'=4,'col'=4] {'row'}, dimensions={0} | all-to-all | bytes 32768 | tf_op jit(solution)/shard_map/all_to_all | solution.py:267
  139.8 6.2 %all_to_all.121.got = f32[4,1,1024]{2,1,0:T(1,128)S(1)} all-to-all(f32[4,1,1024]{2,1,0:T(1,128)S(1)} %get-tuple-element.81), channel_id=1, replica_groups=mesh['groups'=2,'row'=4,'col'=4] {'col'}, dimensions={0} | all-to-all | bytes 32768 | tf_op jit(solution)/shard_map/all_to_all | solution.py:267
  146.9 8.0 %all_to_all.122.got = f32[4,1,1024]{2,1,0:T(1,128)S(1)} all-to-all(f32[4,1,1024]{2,1,0:T(1,128)S(1)} %get-tuple-element.86), channel_id=1, replica_groups=mesh['groups'=2,'row'=4,'col'=4] {'row'}, dimensions={0} | all-to-all | bytes 32768 | tf_op jit(solution)/shard_map/all_to_all | solution.py:267
  155.8 6.2 %all_to_all.123.refs_19_ = f32[4,1,1024]{2,1,0:T(1,128)S(1)} all-to-all(f32[4,1,1024]{2,1,0:T(1,128)S(1)} %get-tuple-element.91), channel_id=1, replica_groups=mesh['groups'=2,'row'=4,'col'=4] {'col'}, dimensions={0} | all-to-all | bytes 32768 | tf_op jit(solution)/shard_map/all_to_all | solution.py:267
  162.0 4.3 %shard_map.60 = (f32[4,32,256]{2,1,0:T(8,128)S(1)}, f32[4,32,256]{2,1,0:T(8,128)}) custom-call(bf16[1024,128]{1,0:T(8,128)(2,1)S(1)} %get-tuple-element.48.left0.ax0, f32[1024,128]{1,0:T(8,128)S(1)} %get-tuple-element.49.left1.ax1, bf16[256,1024]{1,0:T(8,128)(2,1)S(1)} %get-tuple-element.50.right.by, f32[32,1024]{1,0:T(8,128)S(1)} %bitcast.5, ...), custom_call_target="tpu_custom_call" | custom-call | tf_op jit(solution)/shard_map/pallas_call | solution.py:330
  166.3 7.0 %all_to_all.124 = f32[4,32,256]{2,1,0:T(8,128)S(1)} all-to-all(f32[4,32,256]{2,1,0:T(8,128)S(1)} %get-tuple-element.92), channel_id=1, replica_groups=mesh['groups'=2,'row'=4,'col'=4] {'col'}, dimensions={0} | all-to-all | bytes 262144 | tf_op jit(solution)/shard_map/all_to_all | solution.py:267
  173.3 3.3 %all-to-all-start.20 = ((f32[4,32,256]{2,1,0:T(8,128)}), f32[4,32,256]{2,1,0:T(8,128)S(1)}, u32[]{:S(2)}, u32[]{:S(2)}) async-start(f32[4,32,256]{2,1,0:T(8,128)} %get-tuple-element.93), calls=%async_computation.20 | async-start | bytes 262144 | tf_op jit(solution)/shard_map/all_to_all | solution.py:267
  177.3 5.4 %all-to-all-done.20 = f32[4,32,256]{2,1,0:T(8,128)S(1)} async-done(((f32[4,32,256]{2,1,0:T(8,128)}), f32[4,32,256]{2,1,0:T(8,128)S(1)}, u32[]{:S(2)}, u32[]{:S(2)}) %all-to-all-start.20) | async-done | bytes 131104 | tf_op jit(solution)/shard_map/all_to_all | solution.py:267
  (16 shorter events, 12.5 us)
Async XLA Ops:
  0.6 0.9 copy-start
  1.5 0.9 copy-start.1
  173.3 9.4 %all-to-all-start.20 = ((f32[4,32,256]{2,1,0:T(8,128)}), f32[4,32,256]{2,1,0:T(8,128)S(1)}, u32[]{:S(2)}, u32[]{:S(2)}) async-start(f32[4,32,256]{2,1,0:T(8,128)} %get-tuple-element.93), calls=%async_computation.20 | async-start | bytes 262144 | tf_op jit(solution)/shard_map/all_to_all | solution.py:267

commit v3 on v2

--- a/solution.py
+++ b/solution.py
@@ -115,11 +115,6 @@
     return jnp.dot(a, b, preferred_element_type=F32)
 
 
-def send(out, at, wide, value):
-    for d in range(out.shape[0]):
-        out[d, :, at : at + wide] = value
-
-
 def partial_lse(left, right, out):
     width = right.shape[1]
     rows = right_rows(jnp.zeros((1, width), F32))
@@ -128,22 +123,26 @@
         scores = matmul(left, right_chunk(right, rows, at, wide))
         top = jnp.max(scores, axis=0, keepdims=True)
         total = jnp.sum(jnp.exp2(scores - top), axis=0, keepdims=True)
-        send(out, at, wide, top + jnp.log2(total))
-
-
-def join_lse(got, log_mass):
-    parts = [got[d] for d in range(got.shape[0])]
+        out[:, at : at + wide] = top + jnp.log2(total)
+
+
+def join_lse(parts):
+    parts = [p[...] for p in parts]
     top = functools.reduce(jnp.maximum, parts)
-    total = sum(jnp.exp2(p - top) for p in parts)
-    return log_mass - (top + jnp.log2(total))
-
-
-def join_sum(got):
-    return sum(got[d] for d in range(got.shape[0]))
-
-
-def forward_body(log_mass, left0, left1, right, got, pot_out, out):
-    pot = join_lse(got, log_mass)
+    return top + jnp.log2(sum(jnp.exp2(p - top) for p in parts))
+
+
+def join_sum(parts):
+    return sum(p[...] for p in parts)
+
+
+def join_body(join, *refs):
+    refs[-1][...] = join(refs[:-1])
+
+
+def forward_body(log_mass, left0, left1, right, *refs):
+    got, (pot_out, out) = refs[:-2], refs[-2:]
+    pot = log_mass - join_lse(got)
     pot_out[...] = pot
     left, unused = left_factor(left0, left1, pot)
     partial_lse(left, right, out)
@@ -154,17 +153,19 @@
     wide = min(CHUNK, width)
     for at in range(0, width, wide):
         scores = matmul(left, right_chunk(right, rows, at, wide))
-        send(out, at, wide, jnp.sum(jnp.exp2(scores) * column, axis=0, keepdims=True))
-
-
-def turn_body(log_mass, log_scale, left0, left1, right, pot_right, got, pot_out, out):
-    pot = join_lse(got, log_mass)
+        out[:, at : at + wide] = jnp.sum(jnp.exp2(scores) * column, axis=0, keepdims=True)
+
+
+def turn_body(log_mass, log_scale, left0, left1, right, pot_right, *refs):
+    got, (pot_out, out) = refs[:-2], refs[-2:]
+    pot = log_mass - join_lse(got)
     pot_out[...] = pot
     left, column = left_factor(left0, left1, pot, jnp.ones_like(pot))
     weighted_sums(left, column, right, right_rows(pot_right[...] + log_scale), out)
 
 
-def backward_body(leading, log_scale, left0, left1, right, pot_left, pot_right, got, adj_out, out):
+def backward_body(leading, log_scale, left0, left1, right, pot_left, pot_right, *refs):
+    got, (adj_out, out) = refs[:-2], refs[-2:]
     adj = leading - join_sum(got)
     adj_out[...] = adj
     left, column = left_factor(left0, left1, pot_left[...], adj)
@@ -175,12 +176,15 @@
 STRIP = 256
 
 
-def gradient_body(dim, log_cols, log_rows, ax0, ax1, by, x_ref, y_ref, *refs):
+def gradient_body(dim, log_cols, log_rows, n_got, n_col, n_row, ax0, ax1, by, x_ref, y_ref, *refs):
     pots_rows = refs[:ITERS]
     pots_cols = refs[ITERS : 2 * ITERS + 1]
     adjs_rows = refs[2 * ITERS + 1 : 3 * ITERS]
     adjs_cols = refs[3 * ITERS : 4 * ITERS - 1]
-    got, out_x, out_y, cols_rows, x_parts, y_parts, gx, gy, left_e, left_r, right_r = refs[4 * ITERS - 1 :]
+    refs = refs[4 * ITERS - 1 :]
+    got, refs = refs[:n_got], refs[n_got:]
+    outs_x, outs_y = refs[:n_col], refs[n_col : n_col + n_row]
+    cols_rows, x_parts, y_parts, gx, gy, left_e, left_r, right_r, all_x, all_y = refs[n_col + n_row :]
     count_rows, count_cols = x_ref.shape[1], y_ref.shape[1]
     us = [p[...] for p in pots_rows]
     vs = [p[...] for p in pots_cols]
@@ -257,14 +261,38 @@
         mixed = sums[0:dim] + sums[dim : 2 * dim] + sums[2 * dim : 3 * dim]
         return 2.0 * (points * sums[3 * dim : 3 * dim + 1] - mixed)
 
-    for value, out in ((finish(x, gx[...].T), out_x), (finish(y, gy[...]), out_y)):
-        share = out.shape[2]
-        for p in range(out.shape[0]):
-            out[p] = value[:, p * share : (p + 1) * share]
-
-
-def exchange(value, axis):
-    return lax.all_to_all(value, axis, 0, 0, tiled=True)
+    for value, held, outs, axis in (
+        (finish(x, gx[...].T), all_x, outs_x, "col"),
+        (finish(y, gy[...]), all_y, outs_y, "row"),
+    ):
+        share = held.shape[2]
+        for p in range(held.shape[0]):
+            held[p] = value[:, p * share : (p + 1) * share]
+        me = lax.axis_index(axis)
+        for s, out in enumerate(outs):
+            out[...] = held[me ^ s]
+
+
+def swap(value, axis, distance):
+    return lax.ppermute(value, axis, [(d, d ^ distance) for d in range(lax.axis_size(axis))])
+
+
+def exchange(part, axis, join):
+    size = lax.axis_size(axis)
+    assert size & (size - 1) == 0
+    distance = 1
+    got = (part,)
+    while distance < size:
+        if len(got) > 1:
+            (part,) = call(functools.partial(join_body, join), [shape(part.shape)], len(got))(*got)
+        got = (part, swap(part, axis, distance))
+        distance *= 2
+    return got
+
+
+def scatter(pieces, axis):
+    got = [pieces[0]] + [swap(pieces[s], axis, s) for s in range(1, len(pieces))]
+    return sum(got[1:], got[0])
 
 
 def on_device(x_points, y_points):
@@ -276,9 +304,8 @@
     log_rows = math.log2(count_rows * n_row)
     log_cols = math.log2(count_cols * n_col)
     row, col = (1, count_rows), (1, count_cols)
-    to_col, to_row = shape((n_col,) + row), shape((n_row,) + col)
-
-    ax0, ax1, ay0, ay1, bx, by, start, part = pl.pallas_call(
+
+    ax0, ax1, ay0, ay1, bx, by, start, part, x, y = pl.pallas_call(
         prepare_body,
         out_shape=[
             shape((count_rows, 128), BF16),
@@ -288,49 +315,54 @@
             shape((DEPTH, count_rows), BF16),
             shape((DEPTH, count_cols), BF16),
             shape(col),
-            to_col,
+            shape(row),
+            shape(x.shape),
+            shape(y.shape),
         ],
-        in_specs=[pl.BlockSpec(memory_space=pl.ANY)] * 2,
-        out_specs=vmem(8),
-        scratch_shapes=[pltpu.VMEM(x.shape, F32), pltpu.VMEM(y.shape, F32), pltpu.SemaphoreType.DMA((2,))],
+        in_specs=[pl.BlockSpec(memory_space=pltpu.HBM)] * 2,
+        out_specs=vmem(10),
+        scratch_shapes=[pltpu.SemaphoreType.DMA((2,))],
         compiler_params=pltpu.CompilerParams(vmem_limit_bytes=VMEM_LIMIT),
     )(x, y)
 
     pots_rows, pots_cols = [], [start]
     for k in range(ITERS):
-        got = exchange(part, "col")
-        pot, part = call(functools.partial(forward_body, -log_rows), [shape(row), to_row], 4)(ax0, ax1, by, got)
+        got = exchange(part, "col", join_lse)
+        pot, part = call(functools.partial(forward_body, -log_rows), [shape(row), shape(col)], 3 + len(got))(
+            ax0, ax1, by, *got
+        )
         pots_rows.append(pot)
-        got = exchange(part, "row")
+        got = exchange(part, "row", join_lse)
         if k < ITERS - 1:
-            pot, part = call(functools.partial(forward_body, -log_cols), [shape(col), to_col], 4)(
-                ay0, ay1, bx, got
+            pot, part = call(functools.partial(forward_body, -log_cols), [shape(col), shape(row)], 3 + len(got))(
+                ay0, ay1, bx, *got
             )
             pots_cols.append(pot)
-    pot, part = call(functools.partial(turn_body, -log_cols, log_cols), [shape(col), to_col], 5)(
-        ay0, ay1, bx, pots_rows[-1], got
+    pot, part = call(functools.partial(turn_body, -log_cols, log_cols), [shape(col), shape(row)], 4 + len(got))(
+        ay0, ay1, bx, pots_rows[-1], *got
     )
     pots_cols.append(pot)
 
     adjs_rows, adjs_cols = [], []
     for k in reversed(range(1, ITERS)):
         leading = 1.0 if k == ITERS - 1 else 0.0
-        got = exchange(part, "col")
-        adj, part = call(functools.partial(backward_body, leading, log_rows), [shape(row), to_row], 6)(
-            ax0, ax1, by, pots_rows[k], pots_cols[k], got
+        got = exchange(part, "col", join_sum)
+        adj, part = call(functools.partial(backward_body, leading, log_rows), [shape(row), shape(col)], 5 + len(got))(
+            ax0, ax1, by, pots_rows[k], pots_cols[k], *got
         )
         adjs_rows.insert(0, adj)
-        got = exchange(part, "row")
-        adj, part = call(functools.partial(backward_body, 0.0, log_cols), [shape(col), to_col], 6)(
-            ay0, ay1, bx, pots_cols[k], pots_rows[k - 1], got
+        got = exchange(part, "row", join_sum)
+        adj, part = call(functools.partial(backward_body, 0.0, log_cols), [shape(col), shape(row)], 5 + len(got))(
+            ay0, ay1, bx, pots_cols[k], pots_rows[k - 1], *got
         )
         adjs_cols.insert(0, adj)
-    got = exchange(part, "col")
-
-    out_x, out_y = call(
-        functools.partial(gradient_body, dim, log_cols, log_rows),
-        [shape((n_col, dim, count_rows // n_col)), shape((n_row, dim, count_cols // n_row))],
-        5 + 4 * ITERS,
+    got = exchange(part, "col", join_sum)
+
+    share_x, share_y = count_rows // n_col, count_cols // n_row
+    outs = call(
+        functools.partial(gradient_body, dim, log_cols, log_rows, len(got), n_col, n_row),
+        [shape((dim, share_x))] * n_col + [shape((dim, share_y))] * n_row,
+        5 + 4 * ITERS - 1 + len(got),
         [
             pltpu.VMEM((count_rows, 128), F32),
             pltpu.VMEM((128, count_rows), BF16),
@@ -340,10 +372,12 @@
             pltpu.VMEM((count_rows, DEPTH), BF16),
             pltpu.VMEM((count_rows, 128), BF16),
             pltpu.VMEM((128, count_cols), BF16),
+            pltpu.VMEM((n_col, dim, share_x), F32),
+            pltpu.VMEM((n_row, dim, share_y), F32),
         ],
-    )(ax0, ax1, by, x, y, *pots_rows, *pots_cols, *adjs_rows, *adjs_cols, got)
-    grad_x = jnp.sum(exchange(out_x, "col"), axis=0)
-    grad_y = jnp.sum(exchange(out_y, "row"), axis=0)
+    )(ax0, ax1, by, x, y, *pots_rows, *pots_cols, *adjs_rows, *adjs_cols, *got)
+    grad_x = scatter(outs[:n_col], "col")
+    grad_y = scatter(outs[n_col:], "row")
     return (grad_x.T, grad_y.T)
 
 

time: 184 us -> 165 us (0.90)
  blocking collectives: 145 us -> 0 us
  starting transfers between devices: 3.32 us -> 71.8 us
  waiting for transfers between devices: 5.41 us -> 63.4 us
    all_to_all x20 -> x0, blocking collectives: 145 us -> none  [exchange(): return lax.all_to_all(value, axis, 0, 0, tiled=True)]
    ppermute x0 -> x44, starting transfers between devices: none -> 71.8 us  [swap(): lax.ppermute(value, axis, [(d, d ^ distance) for d in range(lax.axis_size...]
    ppermute x0 -> x44, waiting for transfers between devices: none -> 63.4 us  [swap(): lax.ppermute(value, axis, [(d, d ^ distance) for d in range(lax.axis_size...]
    all_to_all x1 -> x0, waiting for transfers between devices: 5.41 us -> none  [exchange(): return lax.all_to_all(value, axis, 0, 0, tiled=True)]
    all_to_all x1 -> x0, starting transfers between devices: 3.32 us -> none  [exchange(): return lax.all_to_all(value, axis, 0, 0, tiled=True)]
    pallas_call x19 -> x38, Pallas kernels: 24.4 us -> 23.8 us  [the longest x5 6.63 us: on_device(): call(functools.partial(forward_body, -log_rows), [shape(row), shape(col)]...]
  transfers between devices with their start and end apart: 1 -> 44, of which waited for: 1 -> 40; matrix products, arithmetic and copies ran while one was open for 0% -> 0% of each run, Pallas kernels for 0% -> 0%
where the time goes in v3:
time: 165 us
  starting transfers between devices  71.8 us (44%)
  waiting for transfers between devices  63.4 us (38%)
  Pallas kernels  25.5 us (15%)
  local copies, waits for them, and re-layouts  1.8 us (1%)
    ppermute x44, starting transfers between devices, swap(): lax.ppermute(value, axis, [(d, d ^ distance) for d in range(lax.axis_size...  71.8 us
    ppermute x44, waiting for transfers between devices, swap(): lax.ppermute(value, axis, [(d, d ^ distance) for d in range(lax.axis_size...  63.4 us
    pallas_call x5, Pallas kernels, on_device(): call(functools.partial(forward_body, -log_rows), [shape(row), shape(col)]...  6.63 us
    pallas_call x4, Pallas kernels, on_device(): call(functools.partial(forward_body, -log_cols), [shape(col), shape(row)]...  5.48 us
    pallas_call x4, Pallas kernels, on_device(): call(functools.partial(backward_body, leading, log_rows), [shape(row), sh...  3.6 us
    pallas_call x4, Pallas kernels, on_device(): call(functools.partial(backward_body, 0.0, log_cols), [shape(col), shape(...  3.57 us
    pallas_call x1, Pallas kernels, on_device(): call(functools.partial(gradient_body, dim, log_cols, log_rows, len(got),...  3.48 us
  transfers between devices with their start and end apart: 44, of which 40 were waited for; matrix products, arithmetic and copies ran while one was open for 0% of the time, Pallas kernels for 0%

profile of v3, /device:TPU:0, one launch (start us, length us, event | category | flops | bytes accessed | tf_op | source)
XLA Modules:
  0.0 164.6 jit_solution(4733197790657365543)
XLA Ops:
  5.5 2.9 %collective-permute-start.1 = (f32[1,1024]{1,0:T(1,128)S(1)}, f32[1,1024]{1,0:T(1,128)S(1)}, u32[]{:S(2)}, u32[]{:S(2)}) collective-permute-start(f32[1,1024]{1,0:T(1,128)S(1)} %shard_map.42.refs_0_), channel_id=1, source_target_pairs={{0,2},{1,3},{2,0},{3,1},{4,6},{5,7},{6,4},{7,5},{8,10},{9,11},{10,... | collective-permute-start | bytes 12296 | tf_op jit(solution)/shard_map/ppermute | solution.py:277
  11.3 2.2 %collective-permute-start.2 = (f32[1,1024]{1,0:T(1,128)S(1)}, f32[1,1024]{1,0:T(1,128)S(1)}, u32[]{:S(2)}, u32[]{:S(2)}) collective-permute-start(f32[1,1024]{1,0:T(1,128)S(1)} %get-tuple-element.66.refs_0_), channel_id=1, source_target_pairs={{0,4},{4,0},{8,12},{12,8},{1,5},{5,1},{9,13},{13,9},{2,6},{6,2},{1... | collective-permute-start | bytes 12296 | tf_op jit(solution)/shard_map/ppermute | solution.py:277
  15.1 3.1 %collective-permute-start.3 = (f32[1,1024]{1,0:T(1,128)S(1)}, f32[1,1024]{1,0:T(1,128)S(1)}, u32[]{:S(2)}, u32[]{:S(2)}) collective-permute-start(f32[1,1024]{1,0:T(1,128)S(1)} %shard_map.44.refs_0_), channel_id=1, source_target_pairs={{0,8},{4,12},{8,0},{12,4},{1,9},{5,13},{9,1},{13,5},{2,10},{6,14},... | collective-permute-start | bytes 12296 | tf_op jit(solution)/shard_map/ppermute | solution.py:277
  22.3 1.9 %collective-permute-start.5 = (f32[1,1024]{1,0:T(1,128)S(1)}, f32[1,1024]{1,0:T(1,128)S(1)}, u32[]{:S(2)}, u32[]{:S(2)}) collective-permute-start(f32[1,1024]{1,0:T(1,128)S(1)} %shard_map.46.refs_0_), channel_id=1, source_target_pairs={{0,2},{1,3},{2,0},{3,1},{4,6},{5,7},{6,4},{7,5},{8,10},{9,11},{10,... | collective-permute-start | bytes 12296 | tf_op jit(solution)/shard_map/ppermute | solution.py:277
  27.3 2.0 %collective-permute-start.6 = (f32[1,1024]{1,0:T(1,128)S(1)}, f32[1,1024]{1,0:T(1,128)S(1)}, u32[]{:S(2)}, u32[]{:S(2)}) collective-permute-start(f32[1,1024]{1,0:T(1,128)S(1)} %get-tuple-element.69.refs_0_), channel_id=1, source_target_pairs={{0,4},{4,0},{8,12},{12,8},{1,5},{5,1},{9,13},{13,9},{2,6},{6,2},{1... | collective-permute-start | bytes 12296 | tf_op jit(solution)/shard_map/ppermute | solution.py:277
  31.0 3.0 %collective-permute-start.7 = (f32[1,1024]{1,0:T(1,128)S(1)}, f32[1,1024]{1,0:T(1,128)S(1)}, u32[]{:S(2)}, u32[]{:S(2)}) collective-permute-start(f32[1,1024]{1,0:T(1,128)S(1)} %shard_map.48.refs_0_), channel_id=1, source_target_pairs={{0,8},{4,12},{8,0},{12,4},{1,9},{5,13},{9,1},{13,5},{2,10},{6,14},... | collective-permute-start | bytes 12296 | tf_op jit(solution)/shard_map/ppermute | solution.py:277
  38.2 1.9 %collective-permute-start.9 = (f32[1,1024]{1,0:T(1,128)S(1)}, f32[1,1024]{1,0:T(1,128)S(1)}, u32[]{:S(2)}, u32[]{:S(2)}) collective-permute-start(f32[1,1024]{1,0:T(1,128)S(1)} %shard_map.50.refs_0_), channel_id=1, source_target_pairs={{0,2},{1,3},{2,0},{3,1},{4,6},{5,7},{6,4},{7,5},{8,10},{9,11},{10,... | collective-permute-start | bytes 12296 | tf_op jit(solution)/shard_map/ppermute | solution.py:277
  43.2 2.0 %collective-permute-start.10 = (f32[1,1024]{1,0:T(1,128)S(1)}, f32[1,1024]{1,0:T(1,128)S(1)}, u32[]{:S(2)}, u32[]{:S(2)}) collective-permute-start(f32[1,1024]{1,0:T(1,128)S(1)} %get-tuple-element.72.refs_0_), channel_id=1, source_target_pairs={{0,4},{4,0},{8,12},{12,8},{1,5},{5,1},{9,13},{13,9},{2,6},{6,2},{1... | collective-permute-start | bytes 12296 | tf_op jit(solution)/shard_map/ppermute | solution.py:277
  46.8 3.0 %collective-permute-start.11 = (f32[1,1024]{1,0:T(1,128)S(1)}, f32[1,1024]{1,0:T(1,128)S(1)}, u32[]{:S(2)}, u32[]{:S(2)}) collective-permute-start(f32[1,1024]{1,0:T(1,128)S(1)} %shard_map.52.refs_0_), channel_id=1, source_target_pairs={{0,8},{4,12},{8,0},{12,4},{1,9},{5,13},{9,1},{13,5},{2,10},{6,14},... | collective-permute-start | bytes 12296 | tf_op jit(solution)/shard_map/ppermute | solution.py:277
  54.0 1.9 %collective-permute-start.13 = (f32[1,1024]{1,0:T(1,128)S(1)}, f32[1,1024]{1,0:T(1,128)S(1)}, u32[]{:S(2)}, u32[]{:S(2)}) collective-permute-start(f32[1,1024]{1,0:T(1,128)S(1)} %shard_map.54.refs_0_), channel_id=1, source_target_pairs={{0,2},{1,3},{2,0},{3,1},{4,6},{5,7},{6,4},{7,5},{8,10},{9,11},{10,... | collective-permute-start | bytes 12296 | tf_op jit(solution)/shard_map/ppermute | solution.py:277
  59.0 2.0 %collective-permute-start.14 = (f32[1,1024]{1,0:T(1,128)S(1)}, f32[1,1024]{1,0:T(1,128)S(1)}, u32[]{:S(2)}, u32[]{:S(2)}) collective-permute-start(f32[1,1024]{1,0:T(1,128)S(1)} %get-tuple-element.75.refs_0_), channel_id=1, source_target_pairs={{0,4},{4,0},{8,12},{12,8},{1,5},{5,1},{9,13},{13,9},{2,6},{6,2},{1... | collective-permute-start | bytes 12296 | tf_op jit(solution)/shard_map/ppermute | solution.py:277
  62.7 3.0 %collective-permute-start.15 = (f32[1,1024]{1,0:T(1,128)S(1)}, f32[1,1024]{1,0:T(1,128)S(1)}, u32[]{:S(2)}, u32[]{:S(2)}) collective-permute-start(f32[1,1024]{1,0:T(1,128)S(1)} %shard_map.56.refs_0_), channel_id=1, source_target_pairs={{0,8},{4,12},{8,0},{12,4},{1,9},{5,13},{9,1},{13,5},{2,10},{6,14},... | collective-permute-start | bytes 12296 | tf_op jit(solution)/shard_map/ppermute | solution.py:277
  70.0 1.9 %collective-permute-start.17 = (f32[1,1024]{1,0:T(1,128)S(1)}, f32[1,1024]{1,0:T(1,128)S(1)}, u32[]{:S(2)}, u32[]{:S(2)}) collective-permute-start(f32[1,1024]{1,0:T(1,128)S(1)} %shard_map.58.refs_0_), channel_id=1, source_target_pairs={{0,2},{1,3},{2,0},{3,1},{4,6},{5,7},{6,4},{7,5},{8,10},{9,11},{10,... | collective-permute-start | bytes 12296 | tf_op jit(solution)/shard_map/ppermute | solution.py:277
  75.0 2.0 %collective-permute-start.18 = (f32[1,1024]{1,0:T(1,128)S(1)}, f32[1,1024]{1,0:T(1,128)S(1)}, u32[]{:S(2)}, u32[]{:S(2)}) collective-permute-start(f32[1,1024]{1,0:T(1,128)S(1)} %get-tuple-element.83.refs_0_), channel_id=1, source_target_pairs={{0,4},{4,0},{8,12},{12,8},{1,5},{5,1},{9,13},{13,9},{2,6},{6,2},{1... | collective-permute-start | bytes 12296 | tf_op jit(solution)/shard_map/ppermute | solution.py:277
  78.7 3.0 %collective-permute-start.19 = (f32[1,1024]{1,0:T(1,128)S(1)}, f32[1,1024]{1,0:T(1,128)S(1)}, u32[]{:S(2)}, u32[]{:S(2)}) collective-permute-start(f32[1,1024]{1,0:T(1,128)S(1)} %shard_map.60.refs_0_), channel_id=1, source_target_pairs={{0,8},{4,12},{8,0},{12,4},{1,9},{5,13},{9,1},{13,5},{2,10},{6,14},... | collective-permute-start | bytes 12296 | tf_op jit(solution)/shard_map/ppermute | solution.py:277
  89.9 2.0 %collective-permute-start.22 = (f32[1,1024]{1,0:T(1,128)S(1)}, f32[1,1024]{1,0:T(1,128)S(1)}, u32[]{:S(2)}, u32[]{:S(2)}) collective-permute-start(f32[1,1024]{1,0:T(1,128)S(1)} %get-tuple-element.86.refs_0_), channel_id=1, source_target_pairs={{0,4},{4,0},{8,12},{12,8},{1,5},{5,1},{9,13},{13,9},{2,6},{6,2},{1... | collective-permute-start | bytes 12296 | tf_op jit(solution)/shard_map/ppermute | solution.py:277
  93.6 2.9 %collective-permute-start.23 = (f32[1,1024]{1,0:T(1,128)S(1)}, f32[1,1024]{1,0:T(1,128)S(1)}, u32[]{:S(2)}, u32[]{:S(2)}) collective-permute-start(f32[1,1024]{1,0:T(1,128)S(1)} %shard_map.64.refs_0_), channel_id=1, source_target_pairs={{0,8},{4,12},{8,0},{12,4},{1,9},{5,13},{9,1},{13,5},{2,10},{6,14},... | collective-permute-start | bytes 12296 | tf_op jit(solution)/shard_map/ppermute | solution.py:277
  100.2 1.8 %collective-permute-start.25 = (f32[1,1024]{1,0:T(1,128)S(1)}, f32[1,1024]{1,0:T(1,128)S(1)}, u32[]{:S(2)}, u32[]{:S(2)}) collective-permute-start(f32[1,1024]{1,0:T(1,128)S(1)} %shard_map.66.refs_0_), channel_id=1, source_target_pairs={{0,2},{1,3},{2,0},{3,1},{4,6},{5,7},{6,4},{7,5},{8,10},{9,11},{10,... | collective-permute-start | bytes 12296 | tf_op jit(solution)/shard_map/ppermute | solution.py:277
  104.8 2.0 %collective-permute-start.26 = (f32[1,1024]{1,0:T(1,128)S(1)}, f32[1,1024]{1,0:T(1,128)S(1)}, u32[]{:S(2)}, u32[]{:S(2)}) collective-permute-start(f32[1,1024]{1,0:T(1,128)S(1)} %get-tuple-element.88.refs_0_), channel_id=1, source_target_pairs={{0,4},{4,0},{8,12},{12,8},{1,5},{5,1},{9,13},{13,9},{2,6},{6,2},{1... | collective-permute-start | bytes 12296 | tf_op jit(solution)/shard_map/ppermute | solution.py:277
  108.4 2.9 %collective-permute-start.27 = (f32[1,1024]{1,0:T(1,128)S(1)}, f32[1,1024]{1,0:T(1,128)S(1)}, u32[]{:S(2)}, u32[]{:S(2)}) collective-permute-start(f32[1,1024]{1,0:T(1,128)S(1)} %shard_map.68.refs_0_), channel_id=1, source_target_pairs={{0,8},{4,12},{8,0},{12,4},{1,9},{5,13},{9,1},{13,5},{2,10},{6,14},... | collective-permute-start | bytes 12296 | tf_op jit(solution)/shard_map/ppermute | solution.py:277
  115.1 1.8 %collective-permute-start.29 = (f32[1,1024]{1,0:T(1,128)S(1)}, f32[1,1024]{1,0:T(1,128)S(1)}, u32[]{:S(2)}, u32[]{:S(2)}) collective-permute-start(f32[1,1024]{1,0:T(1,128)S(1)} %shard_map.70.refs_0_), channel_id=1, source_target_pairs={{0,2},{1,3},{2,0},{3,1},{4,6},{5,7},{6,4},{7,5},{8,10},{9,11},{10,... | collective-permute-start | bytes 12296 | tf_op jit(solution)/shard_map/ppermute | solution.py:277
  119.6 2.0 %collective-permute-start.30 = (f32[1,1024]{1,0:T(1,128)S(1)}, f32[1,1024]{1,0:T(1,128)S(1)}, u32[]{:S(2)}, u32[]{:S(2)}) collective-permute-start(f32[1,1024]{1,0:T(1,128)S(1)} %get-tuple-element.90.refs_0_), channel_id=1, source_target_pairs={{0,4},{4,0},{8,12},{12,8},{1,5},{5,1},{9,13},{13,9},{2,6},{6,2},{1... | collective-permute-start | bytes 12296 | tf_op jit(solution)/shard_map/ppermute | solution.py:277
  123.3 2.9 %collective-permute-start.31 = (f32[1,1024]{1,0:T(1,128)S(1)}, f32[1,1024]{1,0:T(1,128)S(1)}, u32[]{:S(2)}, u32[]{:S(2)}) collective-permute-start(f32[1,1024]{1,0:T(1,128)S(1)} %shard_map.72.refs_0_), channel_id=1, source_target_pairs={{0,8},{4,12},{8,0},{12,4},{1,9},{5,13},{9,1},{13,5},{2,10},{6,14},... | collective-permute-start | bytes 12296 | tf_op jit(solution)/shard_map/ppermute | solution.py:277
  129.9 1.8 %collective-permute-start.33 = (f32[1,1024]{1,0:T(1,128)S(1)}, f32[1,1024]{1,0:T(1,128)S(1)}, u32[]{:S(2)}, u32[]{:S(2)}) collective-permute-start(f32[1,1024]{1,0:T(1,128)S(1)} %shard_map.74.refs_0_), channel_id=1, source_target_pairs={{0,2},{1,3},{2,0},{3,1},{4,6},{5,7},{6,4},{7,5},{8,10},{9,11},{10,... | collective-permute-start | bytes 12296 | tf_op jit(solution)/shard_map/ppermute | solution.py:277
  134.4 2.0 %collective-permute-start.34 = (f32[1,1024]{1,0:T(1,128)S(1)}, f32[1,1024]{1,0:T(1,128)S(1)}, u32[]{:S(2)}, u32[]{:S(2)}) collective-permute-start(f32[1,1024]{1,0:T(1,128)S(1)} %get-tuple-element.96.refs_0_), channel_id=1, source_target_pairs={{0,4},{4,0},{8,12},{12,8},{1,5},{5,1},{9,13},{13,9},{2,6},{6,2},{1... | collective-permute-start | bytes 12296 | tf_op jit(solution)/shard_map/ppermute | solution.py:277
  138.1 2.9 %collective-permute-start.35 = (f32[1,1024]{1,0:T(1,128)S(1)}, f32[1,1024]{1,0:T(1,128)S(1)}, u32[]{:S(2)}, u32[]{:S(2)}) collective-permute-start(f32[1,1024]{1,0:T(1,128)S(1)} %shard_map.76.refs_0_), channel_id=1, source_target_pairs={{0,8},{4,12},{8,0},{12,4},{1,9},{5,13},{9,1},{13,5},{2,10},{6,14},... | collective-permute-start | bytes 12296 | tf_op jit(solution)/shard_map/ppermute | solution.py:277
  144.8 1.8 %collective-permute-start.37 = (f32[1,1024]{1,0:T(1,128)S(1)}, f32[1,1024]{1,0:T(1,128)S(1)}, u32[]{:S(2)}, u32[]{:S(2)}) collective-permute-start(f32[1,1024]{1,0:T(1,128)S(1)} %shard_map.78.refs_19_), channel_id=1, source_target_pairs={{0,2},{1,3},{2,0},{3,1},{4,6},{5,7},{6,4},{7,5},{8,10},{9,11},{10,... | collective-permute-start | bytes 12296 | tf_op jit(solution)/shard_map/ppermute | solution.py:277
  148.4 3.5 %shard_map.79 = (f32[32,256]{1,0:T(8,128)S(1)}, f32[32,256]{1,0:T(8,128)S(1)}, f32[32,256]{1,0:T(8,128)S(1)}, f32[32,256]{1,0:T(8,128)S(1)}, f32[32,256]{1,0:T(8...) custom-call(bf16[1024,128]{1,0:T(8,128)(2,1)S(1)} %get-tuple-element.56.left0.ax0, ...), custom_call_target="tpu_custom_call" | custom-call | tf_op jit(solution)/shard_map/pallas_call | solution.py:362
  151.9 1.9 %collective-permute-start.39 = (f32[32,256]{1,0:T(8,128)S(1)}, f32[32,256]{1,0:T(8,128)S(1)}, u32[]{:S(2)}, u32[]{:S(2)}) collective-permute-start(f32[32,256]{1,0:T(8,128)S(1)} %get-tuple-element.104), channel_id=1, source_target_pairs={{0,2},{1,3},{2,0},{3,1},{4,6},{5,7},{6,4},{7,5},{8,10},{9,11},{10,... | collective-permute-start | bytes 98312 | tf_op jit(solution)/shard_map/ppermute | solution.py:277
  155.7 2.6 %collective-permute-start.42 = (f32[32,256]{1,0:T(8,128)S(1)}, f32[32,256]{1,0:T(8,128)S(1)}, u32[]{:S(2)}, u32[]{:S(2)}) collective-permute-start(f32[32,256]{1,0:T(8,128)S(1)} %get-tuple-element.108), channel_id=1, source_target_pairs={{0,8},{4,12},{8,0},{12,4},{1,9},{5,13},{9,1},{13,5},{2,10},{6,14},... | collective-permute-start | bytes 98312 | tf_op jit(solution)/shard_map/ppermute | solution.py:277
  158.9 2.2 %collective-permute-done.42 = f32[32,256]{1,0:T(8,128)S(1)} collective-permute-done((f32[32,256]{1,0:T(8,128)S(1)}, f32[32,256]{1,0:T(8,128)S(1)}, u32[]{:S(2)}, u32[]{:S(2)}) %collective-permute-start.42) | collective-permute-done | bytes 32800 | tf_op jit(solution)/shard_map/ppermute | solution.py:277
  161.1 2.9 %collective-permute-done.43 = f32[32,256]{1,0:T(8,128)S(1)} collective-permute-done((f32[32,256]{1,0:T(8,128)S(1)}, f32[32,256]{1,0:T(8,128)S(1)}, u32[]{:S(2)}, u32[]{:S(2)}) %collective-permute-start.43) | collective-permute-done | bytes 32800 | tf_op jit(solution)/shard_map/ppermute | solution.py:277
  (101 shorter events, 88.3 us)
Async XLA Ops:
  5.5 4.5 %collective-permute-start.1 = (f32[1,1024]{1,0:T(1,128)S(1)}, f32[1,1024]{1,0:T(1,128)S(1)}, u32[]{:S(2)}, u32[]{:S(2)}) collective-permute-start(f32[1,1024]{1,0:T(1,128)S(1)} %shard_map.42.refs_0_), channel_id=1, source_target_pairs={{0,2},{1,3},{2,0},{3,1},{4,6},{5,7},{6,4},{7,5},{8,10},{9,11},{10,... | collective-permute-start | bytes 12296 | tf_op jit(solution)/shard_map/ppermute | solution.py:277
  11.3 3.8 %collective-permute-start.2 = (f32[1,1024]{1,0:T(1,128)S(1)}, f32[1,1024]{1,0:T(1,128)S(1)}, u32[]{:S(2)}, u32[]{:S(2)}) collective-permute-start(f32[1,1024]{1,0:T(1,128)S(1)} %get-tuple-element.66.refs_0_), channel_id=1, source_target_pairs={{0,4},{4,0},{8,12},{12,8},{1,5},{5,1},{9,13},{13,9},{2,6},{6,2},{1... | collective-permute-start | bytes 12296 | tf_op jit(solution)/shard_map/ppermute | solution.py:277
  15.1 4.7 %collective-permute-start.3 = (f32[1,1024]{1,0:T(1,128)S(1)}, f32[1,1024]{1,0:T(1,128)S(1)}, u32[]{:S(2)}, u32[]{:S(2)}) collective-permute-start(f32[1,1024]{1,0:T(1,128)S(1)} %shard_map.44.refs_0_), channel_id=1, source_target_pairs={{0,8},{4,12},{8,0},{12,4},{1,9},{5,13},{9,1},{13,5},{2,10},{6,14},... | collective-permute-start | bytes 12296 | tf_op jit(solution)/shard_map/ppermute | solution.py:277
  22.3 3.7 %collective-permute-start.5 = (f32[1,1024]{1,0:T(1,128)S(1)}, f32[1,1024]{1,0:T(1,128)S(1)}, u32[]{:S(2)}, u32[]{:S(2)}) collective-permute-start(f32[1,1024]{1,0:T(1,128)S(1)} %shard_map.46.refs_0_), channel_id=1, source_target_pairs={{0,2},{1,3},{2,0},{3,1},{4,6},{5,7},{6,4},{7,5},{8,10},{9,11},{10,... | collective-permute-start | bytes 12296 | tf_op jit(solution)/shard_map/ppermute | solution.py:277
  27.3 3.7 %collective-permute-start.6 = (f32[1,1024]{1,0:T(1,128)S(1)}, f32[1,1024]{1,0:T(1,128)S(1)}, u32[]{:S(2)}, u32[]{:S(2)}) collective-permute-start(f32[1,1024]{1,0:T(1,128)S(1)} %get-tuple-element.69.refs_0_), channel_id=1, source_target_pairs={{0,4},{4,0},{8,12},{12,8},{1,5},{5,1},{9,13},{13,9},{2,6},{6,2},{1... | collective-permute-start | bytes 12296 | tf_op jit(solution)/shard_map/ppermute | solution.py:277
  31.0 4.6 %collective-permute-start.7 = (f32[1,1024]{1,0:T(1,128)S(1)}, f32[1,1024]{1,0:T(1,128)S(1)}, u32[]{:S(2)}, u32[]{:S(2)}) collective-permute-start(f32[1,1024]{1,0:T(1,128)S(1)} %shard_map.48.refs_0_), channel_id=1, source_target_pairs={{0,8},{4,12},{8,0},{12,4},{1,9},{5,13},{9,1},{13,5},{2,10},{6,14},... | collective-permute-start | bytes 12296 | tf_op jit(solution)/shard_map/ppermute | solution.py:277
  38.2 3.7 %collective-permute-start.9 = (f32[1,1024]{1,0:T(1,128)S(1)}, f32[1,1024]{1,0:T(1,128)S(1)}, u32[]{:S(2)}, u32[]{:S(2)}) collective-permute-start(f32[1,1024]{1,0:T(1,128)S(1)} %shard_map.50.refs_0_), channel_id=1, source_target_pairs={{0,2},{1,3},{2,0},{3,1},{4,6},{5,7},{6,4},{7,5},{8,10},{9,11},{10,... | collective-permute-start | bytes 12296 | tf_op jit(solution)/shard_map/ppermute | solution.py:277
  43.2 3.7 %collective-permute-start.10 = (f32[1,1024]{1,0:T(1,128)S(1)}, f32[1,1024]{1,0:T(1,128)S(1)}, u32[]{:S(2)}, u32[]{:S(2)}) collective-permute-start(f32[1,1024]{1,0:T(1,128)S(1)} %get-tuple-element.72.refs_0_), channel_id=1, source_target_pairs={{0,4},{4,0},{8,12},{12,8},{1,5},{5,1},{9,13},{13,9},{2,6},{6,2},{1... | collective-permute-start | bytes 12296 | tf_op jit(solution)/shard_map/ppermute | solution.py:277
  46.8 4.6 %collective-permute-start.11 = (f32[1,1024]{1,0:T(1,128)S(1)}, f32[1,1024]{1,0:T(1,128)S(1)}, u32[]{:S(2)}, u32[]{:S(2)}) collective-permute-start(f32[1,1024]{1,0:T(1,128)S(1)} %shard_map.52.refs_0_), channel_id=1, source_target_pairs={{0,8},{4,12},{8,0},{12,4},{1,9},{5,13},{9,1},{13,5},{2,10},{6,14},... | collective-permute-start | bytes 12296 | tf_op jit(solution)/shard_map/ppermute | solution.py:277
  54.0 3.7 %collective-permute-start.13 = (f32[1,1024]{1,0:T(1,128)S(1)}, f32[1,1024]{1,0:T(1,128)S(1)}, u32[]{:S(2)}, u32[]{:S(2)}) collective-permute-start(f32[1,1024]{1,0:T(1,128)S(1)} %shard_map.54.refs_0_), channel_id=1, source_target_pairs={{0,2},{1,3},{2,0},{3,1},{4,6},{5,7},{6,4},{7,5},{8,10},{9,11},{10,... | collective-permute-start | bytes 12296 | tf_op jit(solution)/shard_map/ppermute | solution.py:277
  59.0 3.7 %collective-permute-start.14 = (f32[1,1024]{1,0:T(1,128)S(1)}, f32[1,1024]{1,0:T(1,128)S(1)}, u32[]{:S(2)}, u32[]{:S(2)}) collective-permute-start(f32[1,1024]{1,0:T(1,128)S(1)} %get-tuple-element.75.refs_0_), channel_id=1, source_target_pairs={{0,4},{4,0},{8,12},{12,8},{1,5},{5,1},{9,13},{13,9},{2,6},{6,2},{1... | collective-permute-start | bytes 12296 | tf_op jit(solution)/shard_map/ppermute | solution.py:277
  62.7 4.6 %collective-permute-start.15 = (f32[1,1024]{1,0:T(1,128)S(1)}, f32[1,1024]{1,0:T(1,128)S(1)}, u32[]{:S(2)}, u32[]{:S(2)}) collective-permute-start(f32[1,1024]{1,0:T(1,128)S(1)} %shard_map.56.refs_0_), channel_id=1, source_target_pairs={{0,8},{4,12},{8,0},{12,4},{1,9},{5,13},{9,1},{13,5},{2,10},{6,14},... | collective-permute-start | bytes 12296 | tf_op jit(solution)/shard_map/ppermute | solution.py:277
  70.0 3.7 %collective-permute-start.17 = (f32[1,1024]{1,0:T(1,128)S(1)}, f32[1,1024]{1,0:T(1,128)S(1)}, u32[]{:S(2)}, u32[]{:S(2)}) collective-permute-start(f32[1,1024]{1,0:T(1,128)S(1)} %shard_map.58.refs_0_), channel_id=1, source_target_pairs={{0,2},{1,3},{2,0},{3,1},{4,6},{5,7},{6,4},{7,5},{8,10},{9,11},{10,... | collective-permute-start | bytes 12296 | tf_op jit(solution)/shard_map/ppermute | solution.py:277
  75.0 3.7 %collective-permute-start.18 = (f32[1,1024]{1,0:T(1,128)S(1)}, f32[1,1024]{1,0:T(1,128)S(1)}, u32[]{:S(2)}, u32[]{:S(2)}) collective-permute-start(f32[1,1024]{1,0:T(1,128)S(1)} %get-tuple-element.83.refs_0_), channel_id=1, source_target_pairs={{0,4},{4,0},{8,12},{12,8},{1,5},{5,1},{9,13},{13,9},{2,6},{6,2},{1... | collective-permute-start | bytes 12296 | tf_op jit(solution)/shard_map/ppermute | solution.py:277
  78.7 4.6 %collective-permute-start.19 = (f32[1,1024]{1,0:T(1,128)S(1)}, f32[1,1024]{1,0:T(1,128)S(1)}, u32[]{:S(2)}, u32[]{:S(2)}) collective-permute-start(f32[1,1024]{1,0:T(1,128)S(1)} %shard_map.60.refs_0_), channel_id=1, source_target_pairs={{0,8},{4,12},{8,0},{12,4},{1,9},{5,13},{9,1},{13,5},{2,10},{6,14},... | collective-permute-start | bytes 12296 | tf_op jit(solution)/shard_map/ppermute | solution.py:277
  85.4 3.6 %collective-permute-start.21 = (f32[1,1024]{1,0:T(1,128)S(1)}, f32[1,1024]{1,0:T(1,128)S(1)}, u32[]{:S(2)}, u32[]{:S(2)}) collective-permute-start(f32[1,1024]{1,0:T(1,128)S(1)} %shard_map.62.refs_0_), channel_id=1, source_target_pairs={{0,2},{1,3},{2,0},{3,1},{4,6},{5,7},{6,4},{7,5},{8,10},{9,11},{10,... | collective-permute-start | bytes 12296 | tf_op jit(solution)/shard_map/ppermute | solution.py:277
  89.9 3.7 %collective-permute-start.22 = (f32[1,1024]{1,0:T(1,128)S(1)}, f32[1,1024]{1,0:T(1,128)S(1)}, u32[]{:S(2)}, u32[]{:S(2)}) collective-permute-start(f32[1,1024]{1,0:T(1,128)S(1)} %get-tuple-element.86.refs_0_), channel_id=1, source_target_pairs={{0,4},{4,0},{8,12},{12,8},{1,5},{5,1},{9,13},{13,9},{2,6},{6,2},{1... | collective-permute-start | bytes 12296 | tf_op jit(solution)/shard_map/ppermute | solution.py:277
  93.6 4.5 %collective-permute-start.23 = (f32[1,1024]{1,0:T(1,128)S(1)}, f32[1,1024]{1,0:T(1,128)S(1)}, u32[]{:S(2)}, u32[]{:S(2)}) collective-permute-start(f32[1,1024]{1,0:T(1,128)S(1)} %shard_map.64.refs_0_), channel_id=1, source_target_pairs={{0,8},{4,12},{8,0},{12,4},{1,9},{5,13},{9,1},{13,5},{2,10},{6,14},... | collective-permute-start | bytes 12296 | tf_op jit(solution)/shard_map/ppermute | solution.py:277
  100.2 3.6 %collective-permute-start.25 = (f32[1,1024]{1,0:T(1,128)S(1)}, f32[1,1024]{1,0:T(1,128)S(1)}, u32[]{:S(2)}, u32[]{:S(2)}) collective-permute-start(f32[1,1024]{1,0:T(1,128)S(1)} %shard_map.66.refs_0_), channel_id=1, source_target_pairs={{0,2},{1,3},{2,0},{3,1},{4,6},{5,7},{6,4},{7,5},{8,10},{9,11},{10,... | collective-permute-start | bytes 12296 | tf_op jit(solution)/shard_map/ppermute | solution.py:277
  104.8 3.7 %collective-permute-start.26 = (f32[1,1024]{1,0:T(1,128)S(1)}, f32[1,1024]{1,0:T(1,128)S(1)}, u32[]{:S(2)}, u32[]{:S(2)}) collective-permute-start(f32[1,1024]{1,0:T(1,128)S(1)} %get-tuple-element.88.refs_0_), channel_id=1, source_target_pairs={{0,4},{4,0},{8,12},{12,8},{1,5},{5,1},{9,13},{13,9},{2,6},{6,2},{1... | collective-permute-start | bytes 12296 | tf_op jit(solution)/shard_map/ppermute | solution.py:277
  108.4 4.5 %collective-permute-start.27 = (f32[1,1024]{1,0:T(1,128)S(1)}, f32[1,1024]{1,0:T(1,128)S(1)}, u32[]{:S(2)}, u32[]{:S(2)}) collective-permute-start(f32[1,1024]{1,0:T(1,128)S(1)} %shard_map.68.refs_0_), channel_id=1, source_target_pairs={{0,8},{4,12},{8,0},{12,4},{1,9},{5,13},{9,1},{13,5},{2,10},{6,14},... | collective-permute-start | bytes 12296 | tf_op jit(solution)/shard_map/ppermute | solution.py:277
  115.1 3.6 %collective-permute-start.29 = (f32[1,1024]{1,0:T(1,128)S(1)}, f32[1,1024]{1,0:T(1,128)S(1)}, u32[]{:S(2)}, u32[]{:S(2)}) collective-permute-start(f32[1,1024]{1,0:T(1,128)S(1)} %shard_map.70.refs_0_), channel_id=1, source_target_pairs={{0,2},{1,3},{2,0},{3,1},{4,6},{5,7},{6,4},{7,5},{8,10},{9,11},{10,... | collective-permute-start | bytes 12296 | tf_op jit(solution)/shard_map/ppermute | solution.py:277
  119.6 3.7 %collective-permute-start.30 = (f32[1,1024]{1,0:T(1,128)S(1)}, f32[1,1024]{1,0:T(1,128)S(1)}, u32[]{:S(2)}, u32[]{:S(2)}) collective-permute-start(f32[1,1024]{1,0:T(1,128)S(1)} %get-tuple-element.90.refs_0_), channel_id=1, source_target_pairs={{0,4},{4,0},{8,12},{12,8},{1,5},{5,1},{9,13},{13,9},{2,6},{6,2},{1... | collective-permute-start | bytes 12296 | tf_op jit(solution)/shard_map/ppermute | solution.py:277
  123.3 4.5 %collective-permute-start.31 = (f32[1,1024]{1,0:T(1,128)S(1)}, f32[1,1024]{1,0:T(1,128)S(1)}, u32[]{:S(2)}, u32[]{:S(2)}) collective-permute-start(f32[1,1024]{1,0:T(1,128)S(1)} %shard_map.72.refs_0_), channel_id=1, source_target_pairs={{0,8},{4,12},{8,0},{12,4},{1,9},{5,13},{9,1},{13,5},{2,10},{6,14},... | collective-permute-start | bytes 12296 | tf_op jit(solution)/shard_map/ppermute | solution.py:277
  134.4 3.7 %collective-permute-start.34 = (f32[1,1024]{1,0:T(1,128)S(1)}, f32[1,1024]{1,0:T(1,128)S(1)}, u32[]{:S(2)}, u32[]{:S(2)}) collective-permute-start(f32[1,1024]{1,0:T(1,128)S(1)} %get-tuple-element.96.refs_0_), channel_id=1, source_target_pairs={{0,4},{4,0},{8,12},{12,8},{1,5},{5,1},{9,13},{13,9},{2,6},{6,2},{1... | collective-permute-start | bytes 12296 | tf_op jit(solution)/shard_map/ppermute | solution.py:277
  138.1 4.5 %collective-permute-start.35 = (f32[1,1024]{1,0:T(1,128)S(1)}, f32[1,1024]{1,0:T(1,128)S(1)}, u32[]{:S(2)}, u32[]{:S(2)}) collective-permute-start(f32[1,1024]{1,0:T(1,128)S(1)} %shard_map.76.refs_0_), channel_id=1, source_target_pairs={{0,8},{4,12},{8,0},{12,4},{1,9},{5,13},{9,1},{13,5},{2,10},{6,14},... | collective-permute-start | bytes 12296 | tf_op jit(solution)/shard_map/ppermute | solution.py:277
  151.8 6.4 %collective-permute-start.38 = (f32[32,256]{1,0:T(8,128)S(1)}, f32[32,256]{1,0:T(8,128)S(1)}, u32[]{:S(2)}, u32[]{:S(2)}) collective-permute-start(f32[32,256]{1,0:T(8,128)S(1)} %get-tuple-element.103), channel_id=1, source_target_pairs={{0,1},{1,0},{2,3},{3,2},{4,5},{5,4},{6,7},{7,6},{8,9},{9,8},{10,11... | collective-permute-start | bytes 98312 | tf_op jit(solution)/shard_map/ppermute | solution.py:277
  151.9 6.4 %collective-permute-start.39 = (f32[32,256]{1,0:T(8,128)S(1)}, f32[32,256]{1,0:T(8,128)S(1)}, u32[]{:S(2)}, u32[]{:S(2)}) collective-permute-start(f32[32,256]{1,0:T(8,128)S(1)} %get-tuple-element.104), channel_id=1, source_target_pairs={{0,2},{1,3},{2,0},{3,1},{4,6},{5,7},{6,4},{7,5},{8,10},{9,11},{10,... | collective-permute-start | bytes 98312 | tf_op jit(solution)/shard_map/ppermute | solution.py:277
  153.8 4.5 %collective-permute-start.40 = (f32[32,256]{1,0:T(8,128)S(1)}, f32[32,256]{1,0:T(8,128)S(1)}, u32[]{:S(2)}, u32[]{:S(2)}) collective-permute-start(f32[32,256]{1,0:T(8,128)S(1)} %get-tuple-element.105), channel_id=1, source_target_pairs={{0,3},{1,2},{2,1},{3,0},{4,7},{5,6},{6,5},{7,4},{8,11},{9,10},{10,... | collective-permute-start | bytes 98312 | tf_op jit(solution)/shard_map/ppermute | solution.py:277
  153.9 5.1 %collective-permute-start.41 = (f32[32,256]{1,0:T(8,128)S(1)}, f32[32,256]{1,0:T(8,128)S(1)}, u32[]{:S(2)}, u32[]{:S(2)}) collective-permute-start(f32[32,256]{1,0:T(8,128)S(1)} %get-tuple-element.107), channel_id=1, source_target_pairs={{0,4},{4,0},{8,12},{12,8},{1,5},{5,1},{9,13},{13,9},{2,6},{6,2},{1... | collective-permute-start | bytes 98312 | tf_op jit(solution)/shard_map/ppermute | solution.py:277
  155.7 5.4 %collective-permute-start.42 = (f32[32,256]{1,0:T(8,128)S(1)}, f32[32,256]{1,0:T(8,128)S(1)}, u32[]{:S(2)}, u32[]{:S(2)}) collective-permute-start(f32[32,256]{1,0:T(8,128)S(1)} %get-tuple-element.108), channel_id=1, source_target_pairs={{0,8},{4,12},{8,0},{12,4},{1,9},{5,13},{9,1},{13,5},{2,10},{6,14},... | collective-permute-start | bytes 98312 | tf_op jit(solution)/shard_map/ppermute | solution.py:277
  158.3 5.7 %collective-permute-start.43 = (f32[32,256]{1,0:T(8,128)S(1)}, f32[32,256]{1,0:T(8,128)S(1)}, u32[]{:S(2)}, u32[]{:S(2)}) collective-permute-start(f32[32,256]{1,0:T(8,128)S(1)} %get-tuple-element.109), channel_id=1, source_target_pairs={{0,12},{4,8},{8,4},{12,0},{1,13},{5,9},{9,5},{13,1},{2,14},{6,10},... | collective-permute-start | bytes 98312 | tf_op jit(solution)/shard_map/ppermute | solution.py:277
  (14 other events, 21.4 us)

commit v4 on v3

--- a/solution.py
+++ b/solution.py
@@ -183,14 +183,19 @@
     adjs_cols = refs[3 * ITERS : 4 * ITERS - 1]
     refs = refs[4 * ITERS - 1 :]
     got, refs = refs[:n_got], refs[n_got:]
-    outs_x, outs_y = refs[:n_col], refs[n_col : n_col + n_row]
-    cols_rows, x_parts, y_parts, gx, gy, left_e, left_r, right_r, all_x, all_y = refs[n_col + n_row :]
-    count_rows, count_cols = x_ref.shape[1], y_ref.shape[1]
     us = [p[...] for p in pots_rows]
     vs = [p[...] for p in pots_cols]
     first = (1.0 if ITERS == 1 else 0.0) - join_sum(got)
     adjs_rows = [first] + [a[...] for a in adjs_rows]
-    adjs_cols = [a[...] for a in adjs_cols] + [jnp.ones((1, count_cols), F32)]
+    adjs_cols = [a[...] for a in adjs_cols] + [jnp.ones(vs[0].shape, F32)]
+    gradient(log_cols, log_rows, n_col, n_row, ax0, ax1, by, x_ref, y_ref, us, vs, adjs_rows, adjs_cols, refs)
+
+
+def gradient(log_cols, log_rows, n_col, n_row, ax0, ax1, by, x_ref, y_ref, us, vs, adjs_rows, adjs_cols, refs):
+    outs_x, outs_y = refs[:n_col], refs[n_col : n_col + n_row]
+    cols_rows, x_parts, y_parts, gx, gy, left_e, left_r, right_r, all_x, all_y = refs[n_col + n_row :]
+    dim, count_rows = x_ref.shape
+    count_cols = y_ref.shape[1]
     shift = log_rows - log_cols
 
     x = x_ref[...]
@@ -295,9 +300,289 @@
     return sum(got[1:], got[0])
 
 
+def slot(column, lane, state):
+    return jnp.where(lax.broadcasted_iota(jnp.int32, state.shape, 1) == lane, column, state)
+
+
+def left_strip(left0, left1, at, pot):
+    strip = left1[at, :]
+    for lane, part in enumerate(split3(jnp.broadcast_to(pot, strip.shape))):
+        strip = slot(part, lane, strip)
+    return jnp.concatenate([left0[at, :], strip.astype(BF16)], axis=1)
+
+
+def halves(value):
+    return sum(value[:, p : p + 128] for p in range(0, value.shape[1], 128))
+
+
+def octets(value):
+    return jnp.sum(value.reshape(value.shape[0] // 8, 8, value.shape[1]), axis=0)
+
+
+SWEEP = 256
+
+
+def sweep(left0, left1, right, rows, state, state_out, held, acc, pot_of, first_sum, put, factor):
+    count, wide_all = left0.shape[0], right.shape[1]
+    strip = min(SWEEP, count)
+    acc[...] = jnp.zeros_like(acc)
+
+    def step(index, carry):
+        at = pl.ds(pl.multiple_of(index * strip, strip), strip)
+        old = state[at, :]
+        left = left_strip(left0, left1, at, pot_of(old))
+        sums = None
+        for c in range(0, wide_all, CHUNK):
+            power = jnp.exp2(matmul(left, right_chunk(right, rows, c, CHUNK)))
+            held[:, c : c + CHUNK] = power
+            part = halves(first_sum(power, c))
+            sums = part if sums is None else sums + part
+        column = jnp.sum(sums, axis=1, keepdims=True)
+        state_out[at, :] = put(old, column)
+        times = factor(old, column)
+        for c in range(0, wide_all, CHUNK):
+            acc[:, c : c + CHUNK] += octets(held[:, c : c + CHUNK] * times)
+        return carry
+
+    lax.fori_loop(0, count // strip, step, 0)
+
+
+def gather_body(n_x, n_y, *refs):
+    xs, ys = refs[:n_x], refs[n_x : n_x + n_y]
+    ay0, ay1, bx, state, out = refs[n_x + n_y :]
+    x = jnp.concatenate([r[...] for r in xs], axis=1)
+    y = jnp.concatenate([r[...] for r in ys], axis=1)
+    bx[...] = factors(x * (2.0 * SCALE), X_ORDER).astype(BF16)
+    turned = factors(y, Y_ORDER).T
+    start = -SCALE * jnp.sum(y * y, axis=0, keepdims=True)
+    ay0[...] = turned[:, :128].astype(BF16)
+    wide = y.shape[1]
+    high, mid, low = split3(start)
+    one = jnp.ones((3, wide), F32)
+    extra = jnp.concatenate([high, mid, low, one, jnp.zeros((122, wide), F32)], axis=0).T
+    with_start = turned[:, 128:] + jnp.where(lax.broadcasted_iota(jnp.int32, extra.shape, 1) < 3, extra, 0.0)
+    ay1[...] = turned[:, 128:] + jnp.where(lax.broadcasted_iota(jnp.int32, extra.shape, 1) < 3, 0.0, extra)
+    state[...] = jnp.concatenate([start, jnp.zeros((127, wide), F32)], axis=0).T
+    left = jnp.concatenate([ay0[...], with_start.astype(BF16)], axis=1)
+    one = jnp.concatenate([jnp.ones((3, CHUNK), F32), jnp.zeros((13, CHUNK), F32)], axis=0).astype(BF16)
+
+    def step(index, carry):
+        at = pl.ds(pl.multiple_of(index * CHUNK, CHUNK), CHUNK)
+        full = jnp.concatenate([bx[0:128, at], one, bx[144:DEPTH, at]], axis=0)
+        scores = matmul(left, full)
+        top = jnp.max(scores, axis=0, keepdims=True)
+        out[:, at] = top + jnp.log2(jnp.sum(jnp.exp2(scores - top), axis=0, keepdims=True))
+        return carry
+
+    lax.fori_loop(0, bx.shape[1] // CHUNK, step, 0)
+
+
+def opening_body(n_got, log_rows, log_cols, left0, left1, right, state, *refs):
+    got, (u_out, state_out, out, held, acc) = refs[:n_got], refs[n_got:]
+    u = -log_rows - join_lse(got)
+    u_out[...] = u
+    rows = right_rows(u)
+    count, wide_all = left0.shape[0], right.shape[1]
+    strip = min(SWEEP, count)
+    acc[...] = jnp.zeros_like(acc)
+
+    def step(index, carry):
+        at = pl.ds(pl.multiple_of(index * strip, strip), strip)
+        left = jnp.concatenate([left0[at, :], left1[at, :].astype(BF16)], axis=1)
+        tops = None
+        for c in range(0, wide_all, CHUNK):
+            scores = matmul(left, right_chunk(right, rows, c, CHUNK))
+            held[:, c : c + CHUNK] = scores
+            part = functools.reduce(jnp.maximum, [scores[:, p : p + 128] for p in range(0, CHUNK, 128)])
+            tops = part if tops is None else jnp.maximum(tops, part)
+        top = jnp.max(tops, axis=1, keepdims=True)
+        sums = None
+        for c in range(0, wide_all, CHUNK):
+            power = jnp.exp2(held[:, c : c + CHUNK] - top)
+            held[:, c : c + CHUNK] = power
+            part = halves(power)
+            sums = part if sums is None else sums + part
+        column = jnp.sum(sums, axis=1, keepdims=True)
+        state_out[at, :] = slot(-log_cols - (top + jnp.log2(column)), 1, state[at, :])
+        times = 2.0**-log_cols / column
+        for c in range(0, wide_all, CHUNK):
+            acc[:, c : c + CHUNK] += octets(held[:, c : c + CHUNK] * times)
+        return carry
+
+    lax.fori_loop(0, count // strip, step, 0)
+    out[...] = jnp.sum(acc[...], axis=0, keepdims=True)
+
+
+def iteration_body(k, n_got, log_rows, log_cols, left0, left1, right, state, u_old, *refs):
+    got, (u_out, state_out, out, held, acc) = refs[:n_got], refs[n_got:]
+    u = u_old[...] - (log_rows + jnp.log2(join_sum(got)))
+    u_out[...] = u
+
+    def put(old, column):
+        pot = old[:, k - 1 : k] - (log_cols + jnp.log2(column))
+        return slot(2.0**log_cols * column, 8 + k, slot(pot, k, old))
+
+    first = (lambda power, c: power, put, lambda old, column: 2.0**-log_cols / column)
+    sweep(left0, left1, right, right_rows(u), state, state_out, held, acc, lambda old: old[:, k - 1 : k], *first)
+    out[...] = jnp.sum(acc[...], axis=0, keepdims=True)
+
+
+def adjoint_body(k, n_got, log_rows, log_cols, left0, left1, right, state, u_ref, u_before, *refs):
+    got, (adj_out, state_out, out, held, acc) = refs[:n_got], refs[n_got:]
+    if k == ITERS:
+        adj = 1.0 - 2.0**log_cols * join_sum(got)
+    else:
+        adj = -join_sum(got)
+    adj_out[...] = adj
+    u = u_ref[...]
+    shift = 2.0 ** (log_rows - log_cols)
+
+    def put(old, column):
+        return slot(-shift * old[:, 8 + k : 9 + k] * column, 16 + k - 1, old)
+
+    def factor(old, column):
+        sigma = old[:, 8 + k : 9 + k]
+        return -shift * sigma * sigma * column
+
+    first = (lambda power, c: power * adj[:, c : c + CHUNK], put, factor)
+    rows = right_rows(u + log_cols)
+    sweep(left0, left1, right, rows, state, state_out, held, acc, lambda old: old[:, k : k + 1], *first)
+    out[...] = jnp.sum(acc[...], axis=0, keepdims=True) * jnp.exp2(u_before[...] - u)
+
+
+def closing_body(n_got, log_cols, log_rows, n_col, n_row, ax0, ax1, by, x_ref, y_ref, state, *refs):
+    count_rows, count_cols = x_ref.shape[1], y_ref.shape[1]
+    us = [r[:, :count_rows] for r in refs[:ITERS]]
+    adjs_rows = [r[:, :count_rows] for r in refs[ITERS : 2 * ITERS - 1]]
+    refs = refs[2 * ITERS - 1 :]
+    got, refs = refs[:n_got], refs[n_got:]
+    first = -join_sum([r[:, :count_rows] for r in got])
+    turned = state[0:count_cols, :].T
+    vs = [turned[k : k + 1] for k in range(ITERS + 1)]
+    adjs_cols = [turned[16 + k : 17 + k] for k in range(1, ITERS)] + [jnp.ones((1, count_cols), F32)]
+    adjs_rows = [first] + adjs_rows
+    gradient(log_cols, log_rows, n_col, n_row, ax0, ax1, by, x_ref, y_ref, us, vs, adjs_rows, adjs_cols, refs)
+
+
+def own_body(x_hbm, y_hbm, ax0, ax1, by, x_ref, y_ref, sems):
+    copies = [
+        pltpu.make_async_copy(x_hbm, x_ref, sems.at[0]),
+        pltpu.make_async_copy(y_hbm, y_ref, sems.at[1]),
+    ]
+    for copy in copies:
+        copy.start()
+    for copy in copies:
+        copy.wait()
+    turned = factors(x_ref[...] * (2.0 * SCALE), X_ORDER).T
+    ax0[...] = turned[:, :128].astype(BF16)
+    ax1[...] = turned[:, 128:]
+    by[...] = factors(y_ref[...], Y_ORDER).astype(BF16)
+
+
+def gradient_scratch(dim, count_rows, count_cols, n_col, n_row):
+    return [
+        pltpu.VMEM((count_rows, 128), F32),
+        pltpu.VMEM((128, count_rows), BF16),
+        pltpu.VMEM((count_cols, 128), BF16),
+        pltpu.VMEM((count_rows, 128), F32),
+        pltpu.VMEM((128, count_cols), F32),
+        pltpu.VMEM((count_rows, DEPTH), BF16),
+        pltpu.VMEM((count_rows, 128), BF16),
+        pltpu.VMEM((128, count_cols), BF16),
+        pltpu.VMEM((n_col, dim, count_rows // n_col), F32),
+        pltpu.VMEM((n_row, dim, count_cols // n_row), F32),
+    ]
+
+
+CORES = 2
+
+
+def repeated(x, y):
+    dim, count_rows = x.shape
+    count_cols = y.shape[1]
+    n_row, n_col = lax.axis_size("row"), lax.axis_size("col")
+    n_chips = n_col // CORES
+    all_rows, held_cols = count_rows * n_row, count_cols * n_chips
+    log_rows, log_cols = math.log2(all_rows), math.log2(count_cols * n_col)
+    row, col = (1, all_rows), (1, held_cols)
+
+    xs = [x] + [swap(x, "row", s) for s in range(1, n_row)]
+    ys = [y] + [swap(y, "col", s * CORES) for s in range(1, n_chips)]
+    ax0, ax1, by, x, y = pl.pallas_call(
+        own_body,
+        out_shape=[
+            shape((count_rows, 128), BF16),
+            shape((count_rows, 128)),
+            shape((DEPTH, count_cols), BF16),
+            shape(x.shape),
+            shape(y.shape),
+        ],
+        in_specs=[pl.BlockSpec(memory_space=pltpu.HBM)] * 2,
+        out_specs=vmem(5),
+        scratch_shapes=[pltpu.SemaphoreType.DMA((2,))],
+        compiler_params=pltpu.CompilerParams(vmem_limit_bytes=VMEM_LIMIT),
+    )(x, y)
+    ay0, ay1, bx, state, part = call(
+        functools.partial(gather_body, n_row, n_chips),
+        [
+            shape((held_cols, 128), BF16),
+            shape((held_cols, 128)),
+            shape((DEPTH, all_rows), BF16),
+            shape((held_cols, 128)),
+            shape(row),
+        ],
+        n_row + n_chips,
+    )(*xs, *ys)
+
+    strip = min(SWEEP, held_cols)
+    scratch = [pltpu.VMEM((strip, all_rows), F32), pltpu.VMEM((8, all_rows), F32)]
+    results = [shape(row), shape((held_cols, 128)), shape(row)]
+    got = (part, swap(part, "col", 1))
+    us = []
+    u, state, part = call(
+        functools.partial(opening_body, len(got), log_rows, log_cols), results, 4 + len(got), scratch
+    )(ay0, ay1, bx, state, *got)
+    us.append(u)
+    for k in range(2, ITERS + 1):
+        got = (part, swap(part, "col", 1))
+        u, state, part = call(
+            functools.partial(iteration_body, k, len(got), log_rows, log_cols), results, 5 + len(got), scratch
+        )(ay0, ay1, bx, state, u, *got)
+        us.append(u)
+    adjs_rows = []
+    for k in range(ITERS, 1, -1):
+        got = (part, swap(part, "col", 1))
+        adj, state, part = call(
+            functools.partial(adjoint_body, k, len(got), log_rows, log_cols),
+            results,
+            6 + len(got),
+            scratch,
+        )(ay0, ay1, bx, state, us[k - 1], us[k - 2], *got)
+        adjs_rows.insert(0, adj)
+    got = (part, swap(part, "col", 1))
+    outs = call(
+        functools.partial(closing_body, len(got), log_cols, log_rows, n_col, n_row),
+        [shape((dim, count_rows // n_col))] * n_col + [shape((dim, count_cols // n_row))] * n_row,
+        6 + 2 * ITERS - 1 + len(got),
+        gradient_scratch(dim, count_rows, count_cols, n_col, n_row),
+    )(ax0, ax1, by, x, y, state, *us, *adjs_rows, *got)
+    return scatter(outs[:n_col], "col").T, scatter(outs[n_col:], "row").T
+
+
+REPEAT_PAIRS = 1 << 23
+
+
 def on_device(x_points, y_points):
     x = x_points.T
     y = y_points.T
+    n_row, n_col = lax.axis_size("row"), lax.axis_size("col")
+    pairs = x.shape[1] * n_row * y.shape[1] * n_col // CORES
+    if ITERS > 1 and n_col % CORES == 0 and pairs <= REPEAT_PAIRS:
+        return repeated(x, y)
+    return shared(x, y)
+
+
+def shared(x, y):
     dim, count_rows = x.shape
     count_cols = y.shape[1]
     n_row, n_col = lax.axis_size("row"), lax.axis_size("col")
@@ -363,18 +648,7 @@
         functools.partial(gradient_body, dim, log_cols, log_rows, len(got), n_col, n_row),
         [shape((dim, share_x))] * n_col + [shape((dim, share_y))] * n_row,
         5 + 4 * ITERS - 1 + len(got),
-        [
-            pltpu.VMEM((count_rows, 128), F32),
-            pltpu.VMEM((128, count_rows), BF16),
-            pltpu.VMEM((count_cols, 128), BF16),
-            pltpu.VMEM((count_rows, 128), F32),
-            pltpu.VMEM((128, count_cols), F32),
-            pltpu.VMEM((count_rows, DEPTH), BF16),
-            pltpu.VMEM((count_rows, 128), BF16),
-            pltpu.VMEM((128, count_cols), BF16),
-            pltpu.VMEM((n_col, dim, share_x), F32),
-            pltpu.VMEM((n_row, dim, share_y), F32),
-        ],
+        gradient_scratch(dim, count_rows, count_cols, n_col, n_row),
     )(ax0, ax1, by, x, y, *pots_rows, *pots_cols, *adjs_rows, *adjs_cols, *got)
     grad_x = scatter(outs[:n_col], "col")
     grad_y = scatter(outs[n_col:], "row")

time: 165 us -> 151 us (0.915)
  Pallas kernels: 25.5 us -> 111 us
  starting transfers between devices: 71.8 us -> 15.9 us
  waiting for transfers between devices: 63.4 us -> 21.1 us
    pallas_call x39 -> x12, Pallas kernels: 25.5 us -> 111 us  [the longest x4 39.7 us: repeated(): call(functools.partial(adjoint_body, k, len(got), log_rows, log_cols), re...]
    ppermute x44 -> x20, starting transfers between devices: 71.8 us -> 15.9 us  [swap(): lax.ppermute(value, axis, [(d, d ^ distance) for d in range(lax.axis_size...]
    ppermute x44 -> x20, waiting for transfers between devices: 63.4 us -> 21.1 us  [swap(): lax.ppermute(value, axis, [(d, d ^ distance) for d in range(lax.axis_size...]
  transfers between devices with their start and end apart: 44 -> 20, of which waited for: 40 -> 14; matrix products, arithmetic and copies ran while one was open for 0% -> 0% of each run, Pallas kernels for 0% -> 0%
where the time goes in v4:
time: 151 us
  Pallas kernels  111 us (74%)
  waiting for transfers between devices  21.1 us (14%)
  starting transfers between devices  15.9 us (11%)
  local copies, waits for them, and re-layouts  1.81 us (1%)
    pallas_call x4, Pallas kernels, repeated(): call(functools.partial(adjoint_body, k, len(got), log_rows, log_cols), re...  39.7 us
    pallas_call x4, Pallas kernels, repeated(): call(functools.partial(iteration_body, k, len(got), log_rows, log_cols),...  38.1 us
    ppermute x20, waiting for transfers between devices, swap(): lax.ppermute(value, axis, [(d, d ^ distance) for d in range(lax.axis_size...  21.1 us
    ppermute x20, starting transfers between devices, swap(): lax.ppermute(value, axis, [(d, d ^ distance) for d in range(lax.axis_size...  15.9 us
    pallas_call x1, Pallas kernels, repeated(): call(functools.partial(gather_body, n_row, n_chips), [shape((held_cols, 1...  15.6 us
    pallas_call x1, Pallas kernels, repeated(): call(functools.partial(opening_body, len(got), log_rows, log_cols), resul...  12.9 us
    pallas_call x1, Pallas kernels, repeated(): call(functools.partial(closing_body, len(got), log_cols, log_rows, n_col,...  3.61 us
  transfers between devices with their start and end apart: 20, of which 14 were waited for; matrix products, arithmetic and copies ran while one was open for 0% of the time, Pallas kernels for 0%

profile of v4, /device:TPU:0, one launch (start us, length us, event | category | flops | bytes accessed | tf_op | source)
XLA Modules:
  0.0 151.3 jit_solution(15137676663396795947)
XLA Ops:
  0.6 3.1 %collective-permute-start = (f32[32,1024]{1,0:T(8,128)}, f32[32,1024]{1,0:T(8,128)S(1)}, u32[]{:S(2)}, u32[]{:S(2)}) collective-permute-start(f32[32,1024]{1,0:T(8,128)} %bitcast.6), channel_id=1, source_target_pairs={{0,4},{4,0},{8,12},{12,8},{1,5},{5,1},{9,13},{13,9},{2,6},{6,2},{1... | collective-permute-start | bytes 393224 | tf_op jit(solution)/shard_map/ppermute | solution.py:282
  3.7 2.6 %collective-permute-start.1 = (f32[32,1024]{1,0:T(8,128)}, f32[32,1024]{1,0:T(8,128)S(1)}, u32[]{:S(2)}, u32[]{:S(2)}) collective-permute-start(f32[32,1024]{1,0:T(8,128)} %bitcast.7), channel_id=1, source_target_pairs={{0,8},{4,12},{8,0},{12,4},{1,9},{5,13},{9,1},{13,5},{2,10},{6,14},... | collective-permute-start | bytes 393224 | tf_op jit(solution)/shard_map/ppermute | solution.py:282
  6.3 1.7 %collective-permute-start.3 = (f32[32,1024]{1,0:T(8,128)}, f32[32,1024]{1,0:T(8,128)S(1)}, u32[]{:S(2)}, u32[]{:S(2)}) collective-permute-start(f32[32,1024]{1,0:T(8,128)} %bitcast.11), channel_id=1, source_target_pairs={{0,2},{1,3},{2,0},{3,1},{4,6},{5,7},{6,4},{7,5},{8,10},{9,11},{10,... | collective-permute-start | bytes 393224 | tf_op jit(solution)/shard_map/ppermute | solution.py:282
  8.0 0.9 collective-permute-done.refs_1_
  9.0 7.9 %collective-permute-done.1.refs_2_ = f32[32,1024]{1,0:T(8,128)S(1)} collective-permute-done((f32[32,1024]{1,0:T(8,128)}, f32[32,1024]{1,0:T(8,128)S(1)}, u32[]{:S(2)}, u32[]{:S(2)}) %collective-permute-start.1) | collective-permute-done | bytes 131104 | tf_op jit(solution)/shard_map/ppermute | solution.py:282
  16.9 0.9 copy-done
  18.7 15.6 %shard_map.42 = (bf16[2048,128]{1,0:T(8,128)(2,1)S(1)}, f32[2048,128]{1,0:T(8,128)S(1)}, bf16[256,4096]{1,0:T(8,128)(2,1)S(1)}, f32[2048,128]{1,0:T(8,128)S(1)}, f32[1,4096]{1,0:T(1,128)S(1)}) custom-call(f32[32,1024]{1,0:T(8,128)S(1)} %bitcast.9, f32[32,1024]{1,0:T(8,128)S(1)} %collective-permute-done.refs_1_, ...), custom_call_target="tpu_custom_call" | custom-call | tf_op jit(solution)/shard_map/pallas_call | solution.py:525
  34.3 1.2 collective-permute-done.4.refs_1_
  35.5 12.9 %shard_map.43 = (f32[1,4096]{1,0:T(1,128)S(1)}, f32[2048,128]{1,0:T(8,128)S(1)}, f32[1,4096]{1,0:T(1,128)S(1)}) custom-call(bf16[2048,128]{1,0:T(8,128)(2,1)S(1)} %get-tuple-element.52.left0, f32[2048,128]{1,0:T(8,128)S(1)} %get-tuple-element.53.left1, bf16[256,4096]{1,0:T(8,128)(2,1)S(1)} %get-tuple-element.54.right, ...), custom_call_target="tpu_custom_call" | custom-call | tf_op jit(solution)/shard_map/pallas_call | solution.py:542
  48.7 1.0 collective-permute-done.5.refs_1_
  49.7 9.5 %shard_map.44 = (f32[1,4096]{1,0:T(1,128)S(1)}, f32[2048,128]{1,0:T(8,128)S(1)}, f32[1,4096]{1,0:T(1,128)S(1)}) custom-call(bf16[2048,128]{1,0:T(8,128)(2,1)S(1)} %get-tuple-element.52.left0, f32[2048,128]{1,0:T(8,128)S(1)} %get-tuple-element.53.left1, bf16[256,4096]{1,0:T(8,128)(2,1)S(1)} %get-tuple-element.54.right, ...), custom_call_target="tpu_custom_call" | custom-call | tf_op jit(solution)/shard_map/pallas_call | solution.py:548
  59.5 1.0 collective-permute-done.6.refs_1_
  60.5 9.5 %shard_map.45 = (f32[1,4096]{1,0:T(1,128)S(1)}, f32[2048,128]{1,0:T(8,128)S(1)}, f32[1,4096]{1,0:T(1,128)S(1)}) custom-call(bf16[2048,128]{1,0:T(8,128)(2,1)S(1)} %get-tuple-element.52.left0, f32[2048,128]{1,0:T(8,128)S(1)} %get-tuple-element.53.left1, bf16[256,4096]{1,0:T(8,128)(2,1)S(1)} %get-tuple-element.54.right, ...), custom_call_target="tpu_custom_call" | custom-call | tf_op jit(solution)/shard_map/pallas_call | solution.py:548
  70.2 1.0 collective-permute-done.7.refs_1_
  71.3 9.5 %shard_map.46 = (f32[1,4096]{1,0:T(1,128)S(1)}, f32[2048,128]{1,0:T(8,128)S(1)}, f32[1,4096]{1,0:T(1,128)S(1)}) custom-call(bf16[2048,128]{1,0:T(8,128)(2,1)S(1)} %get-tuple-element.52.left0, f32[2048,128]{1,0:T(8,128)S(1)} %get-tuple-element.53.left1, bf16[256,4096]{1,0:T(8,128)(2,1)S(1)} %get-tuple-element.54.right, ...), custom_call_target="tpu_custom_call" | custom-call | tf_op jit(solution)/shard_map/pallas_call | solution.py:548
  81.0 1.0 collective-permute-done.8.refs_1_
  82.0 9.5 %shard_map.47 = (f32[1,4096]{1,0:T(1,128)S(1)}, f32[2048,128]{1,0:T(8,128)S(1)}, f32[1,4096]{1,0:T(1,128)S(1)}) custom-call(bf16[2048,128]{1,0:T(8,128)(2,1)S(1)} %get-tuple-element.52.left0, f32[2048,128]{1,0:T(8,128)S(1)} %get-tuple-element.53.left1, bf16[256,4096]{1,0:T(8,128)(2,1)S(1)} %get-tuple-element.54.right, ...), custom_call_target="tpu_custom_call" | custom-call | tf_op jit(solution)/shard_map/pallas_call | solution.py:548
  91.8 1.0 collective-permute-done.9.refs_1_
  92.8 9.9 %shard_map.48 = (f32[1,4096]{1,0:T(1,128)S(1)}, f32[2048,128]{1,0:T(8,128)S(1)}, f32[1,4096]{1,0:T(1,128)S(1)}) custom-call(bf16[2048,128]{1,0:T(8,128)(2,1)S(1)} %get-tuple-element.52.left0, f32[2048,128]{1,0:T(8,128)S(1)} %get-tuple-element.53.left1, bf16[256,4096]{1,0:T(8,128)(2,1)S(1)} %get-tuple-element.54.right, ...), custom_call_target="tpu_custom_call" | custom-call | tf_op jit(solution)/shard_map/pallas_call | solution.py:555
  103.0 1.0 collective-permute-done.10.refs_1_
  104.0 9.9 %shard_map.49 = (f32[1,4096]{1,0:T(1,128)S(1)}, f32[2048,128]{1,0:T(8,128)S(1)}, f32[1,4096]{1,0:T(1,128)S(1)}) custom-call(bf16[2048,128]{1,0:T(8,128)(2,1)S(1)} %get-tuple-element.52.left0, f32[2048,128]{1,0:T(8,128)S(1)} %get-tuple-element.53.left1, bf16[256,4096]{1,0:T(8,128)(2,1)S(1)} %get-tuple-element.54.right, ...), custom_call_target="tpu_custom_call" | custom-call | tf_op jit(solution)/shard_map/pallas_call | solution.py:555
  114.1 1.0 collective-permute-done.11.refs_1_
  115.1 10.1 %shard_map.50 = (f32[1,4096]{1,0:T(1,128)S(1)}, f32[2048,128]{1,0:T(8,128)S(1)}, f32[1,4096]{1,0:T(1,128)S(1)}) custom-call(bf16[2048,128]{1,0:T(8,128)(2,1)S(1)} %get-tuple-element.52.left0, f32[2048,128]{1,0:T(8,128)S(1)} %get-tuple-element.53.left1, bf16[256,4096]{1,0:T(8,128)(2,1)S(1)} %get-tuple-element.54.right, ...), custom_call_target="tpu_custom_call" | custom-call | tf_op jit(solution)/shard_map/pallas_call | solution.py:555
  125.4 1.0 collective-permute-done.12.refs_1_
  126.4 9.9 %shard_map.51 = (f32[1,4096]{1,0:T(1,128)S(1)}, f32[2048,128]{1,0:T(8,128)S(1)}, f32[1,4096]{1,0:T(1,128)S(1)}) custom-call(bf16[2048,128]{1,0:T(8,128)(2,1)S(1)} %get-tuple-element.52.left0, f32[2048,128]{1,0:T(8,128)S(1)} %get-tuple-element.53.left1, bf16[256,4096]{1,0:T(8,128)(2,1)S(1)} %get-tuple-element.54.right, ...), custom_call_target="tpu_custom_call" | custom-call | tf_op jit(solution)/shard_map/pallas_call | solution.py:555
  137.6 3.6 %shard_map.52 = (f32[32,256]{1,0:T(8,128)S(1)}, f32[32,256]{1,0:T(8,128)S(1)}, f32[32,256]{1,0:T(8,128)S(1)}, f32[32,256]{1,0:T(8,128)S(1)}, f32[32,256]{1,0:T(8...) custom-call(bf16[1024,128]{1,0:T(8,128)(2,1)S(1)} %get-tuple-element.47.ax0, ...), custom_call_target="tpu_custom_call" | custom-call | tf_op jit(solution)/shard_map/pallas_call | solution.py:563
  141.2 2.0 %collective-permute-start.17 = (f32[32,256]{1,0:T(8,128)S(1)}, f32[32,256]{1,0:T(8,128)S(1)}, u32[]{:S(2)}, u32[]{:S(2)}) collective-permute-start(f32[32,256]{1,0:T(8,128)S(1)} %get-tuple-element.89), channel_id=1, source_target_pairs={{0,4},{4,0},{8,12},{12,8},{1,5},{5,1},{9,13},{13,9},{2,6},{6,2},{1... | collective-permute-start | bytes 98312 | tf_op jit(solution)/shard_map/ppermute | solution.py:282
  143.2 1.1 collective-permute-start.18
  144.3 1.4 collective-permute-start.19
  145.7 1.5 collective-permute-start.15
  147.6 1.1 collective-permute-done.18
  148.6 1.4 collective-permute-done.19
  (26 shorter events, 5.7 us)
Async XLA Ops:
  0.6 8.3 %collective-permute-start = (f32[32,1024]{1,0:T(8,128)}, f32[32,1024]{1,0:T(8,128)S(1)}, u32[]{:S(2)}, u32[]{:S(2)}) collective-permute-start(f32[32,1024]{1,0:T(8,128)} %bitcast.6), channel_id=1, source_target_pairs={{0,4},{4,0},{8,12},{12,8},{1,5},{5,1},{9,13},{13,9},{2,6},{6,2},{1... | collective-permute-start | bytes 393224 | tf_op jit(solution)/shard_map/ppermute | solution.py:282
  3.7 13.2 %collective-permute-start.1 = (f32[32,1024]{1,0:T(8,128)}, f32[32,1024]{1,0:T(8,128)S(1)}, u32[]{:S(2)}, u32[]{:S(2)}) collective-permute-start(f32[32,1024]{1,0:T(8,128)} %bitcast.7), channel_id=1, source_target_pairs={{0,8},{4,12},{8,0},{12,4},{1,9},{5,13},{9,1},{13,5},{2,10},{6,14},... | collective-permute-start | bytes 393224 | tf_op jit(solution)/shard_map/ppermute | solution.py:282
  6.3 10.6 %collective-permute-start.2 = (f32[32,1024]{1,0:T(8,128)}, f32[32,1024]{1,0:T(8,128)S(1)}, u32[]{:S(2)}, u32[]{:S(2)}) collective-permute-start(f32[32,1024]{1,0:T(8,128)} %bitcast.8), channel_id=1, source_target_pairs={{0,12},{4,8},{8,4},{12,0},{1,13},{5,9},{9,5},{13,1},{2,14},{6,10},... | collective-permute-start | bytes 393224 | tf_op jit(solution)/shard_map/ppermute | solution.py:282
  6.3 10.6 %collective-permute-start.3 = (f32[32,1024]{1,0:T(8,128)}, f32[32,1024]{1,0:T(8,128)S(1)}, u32[]{:S(2)}, u32[]{:S(2)}) collective-permute-start(f32[32,1024]{1,0:T(8,128)} %bitcast.11), channel_id=1, source_target_pairs={{0,2},{1,3},{2,0},{3,1},{4,6},{5,7},{6,4},{7,5},{8,10},{9,11},{10,... | collective-permute-start | bytes 393224 | tf_op jit(solution)/shard_map/ppermute | solution.py:282
  16.9 0.9 copy-start
  17.8 0.9 copy-start.1
  34.3 1.2 collective-permute-start.4
  48.4 1.2 collective-permute-start.5
  59.2 1.2 collective-permute-start.6
  70.0 1.2 collective-permute-start.7
  80.8 1.2 collective-permute-start.8
  91.6 1.2 collective-permute-start.9
  102.7 1.2 collective-permute-start.10
  113.9 1.2 collective-permute-start.11
  125.2 1.2 collective-permute-start.12
  136.3 1.2 collective-permute-start.13
  141.2 6.0 %collective-permute-start.17 = (f32[32,256]{1,0:T(8,128)S(1)}, f32[32,256]{1,0:T(8,128)S(1)}, u32[]{:S(2)}, u32[]{:S(2)}) collective-permute-start(f32[32,256]{1,0:T(8,128)S(1)} %get-tuple-element.89), channel_id=1, source_target_pairs={{0,4},{4,0},{8,12},{12,8},{1,5},{5,1},{9,13},{13,9},{2,6},{6,2},{1... | collective-permute-start | bytes 98312 | tf_op jit(solution)/shard_map/ppermute | solution.py:282
  143.2 5.4 %collective-permute-start.18 = (f32[32,256]{1,0:T(8,128)S(1)}, f32[32,256]{1,0:T(8,128)S(1)}, u32[]{:S(2)}, u32[]{:S(2)}) collective-permute-start(f32[32,256]{1,0:T(8,128)S(1)} %get-tuple-element.90), channel_id=1, source_target_pairs={{0,8},{4,12},{8,0},{12,4},{1,9},{5,13},{9,1},{13,5},{2,10},{6,14},... | collective-permute-start | bytes 98312 | tf_op jit(solution)/shard_map/ppermute | solution.py:282
  144.3 5.7 %collective-permute-start.19 = (f32[32,256]{1,0:T(8,128)S(1)}, f32[32,256]{1,0:T(8,128)S(1)}, u32[]{:S(2)}, u32[]{:S(2)}) collective-permute-start(f32[32,256]{1,0:T(8,128)S(1)} %get-tuple-element.91), channel_id=1, source_target_pairs={{0,12},{4,8},{8,4},{12,0},{1,13},{5,9},{9,5},{13,1},{2,14},{6,10},... | collective-permute-start | bytes 98312 | tf_op jit(solution)/shard_map/ppermute | solution.py:282
  145.7 5.0 %collective-permute-start.14 = (f32[32,256]{1,0:T(8,128)S(1)}, f32[32,256]{1,0:T(8,128)S(1)}, u32[]{:S(2)}, u32[]{:S(2)}) collective-permute-start(f32[32,256]{1,0:T(8,128)S(1)} %get-tuple-element.85), channel_id=1, source_target_pairs={{0,1},{1,0},{2,3},{3,2},{4,5},{5,4},{6,7},{7,6},{8,9},{9,8},{10,11... | collective-permute-start | bytes 98312 | tf_op jit(solution)/shard_map/ppermute | solution.py:282
  145.7 5.0 %collective-permute-start.15 = (f32[32,256]{1,0:T(8,128)S(1)}, f32[32,256]{1,0:T(8,128)S(1)}, u32[]{:S(2)}, u32[]{:S(2)}) collective-permute-start(f32[32,256]{1,0:T(8,128)S(1)} %get-tuple-element.86), channel_id=1, source_target_pairs={{0,2},{1,3},{2,0},{3,1},{4,6},{5,7},{6,4},{7,5},{8,10},{9,11},{10,... | collective-permute-start | bytes 98312 | tf_op jit(solution)/shard_map/ppermute | solution.py:282
  147.2 3.5 %collective-permute-start.16 = (f32[32,256]{1,0:T(8,128)S(1)}, f32[32,256]{1,0:T(8,128)S(1)}, u32[]{:S(2)}, u32[]{:S(2)}) collective-permute-start(f32[32,256]{1,0:T(8,128)S(1)} %get-tuple-element.87), channel_id=1, source_target_pairs={{0,3},{1,2},{2,1},{3,0},{4,7},{5,6},{6,5},{7,4},{8,11},{9,10},{10,... | collective-permute-start | bytes 98312 | tf_op jit(solution)/shard_map/ppermute | solution.py:282
